TPU v7x, 128 devices: a whole 4x4x4 slice. The times are simulated.
128 devices in a mesh: head: 16 (over x, y_hi, core), seq: 8 (over z, y_lo).
Axes of the slice: x: 4, y: 4 (y_hi: 2, y_lo: 2; y = y_hi * 2 + y_lo), z: 4, core: 2. Of those that a mesh axis runs over, the one named last changes fastest.
Arguments:
- hidden: bfloat16 [2048, 8, 2048], P('head', 'seq'), may hold values from -6 to 6
- memory: bfloat16 [50, 8, 2048], P(None, 'seq'), may hold values from -6 to 6
- counts: int32 [8, 2], P('seq'), may hold values from 20 to 50, as said below
- w_qkv: bfloat16 [2048, 3, 2048], P(None, None, 'head'), may hold values from -0.125 to 0.125
- b_query: float32 [2048], P('head'), may hold values from -3 to 3
- b_value: float32 [2048], P('head'), may hold values from -3 to 3
- output_weight: bfloat16 [2048, 2048], P('head'), may hold values from -1 to 1
- b_out: float32 [2048], replicated, may hold values from -2 to 2
- gain_one: float32 [2048], replicated, may hold values from 0.5 to 1.5
- shift_one: float32 [2048], replicated, may hold values from -2 to 2
- gain_two: float32 [2048], replicated, may hold values from 0.5 to 1.5
- shift_two: float32 [2048], replicated, may hold values from -2 to 2
- w_up: bfloat16 [2048, 8192], P(None, 'seq'), may hold values from -0.125 to 0.125
- up_bias: float32 [8192], replicated, may hold values from -3 to 3
- w_down: bfloat16 [8192, 2048], P('seq'), may hold values from -0.0625 to 0.0625
- b_down: float32 [2048], replicated, may hold values from -2 to 2
- cotangent: bfloat16 [2048, 8, 2048], P('head', 'seq'), may hold values from -6 to 6
Outputs:
- output: bfloat16 [2048, 8, 2048], P('head', 'seq')
- grad_hidden: float32 [2048, 8, 2048], P('head', 'seq')
- grad_memory: float32 [50, 8, 2048], P(None, 'seq')
- grad_w_qkv: float32 [2048, 3, 2048], P(None, None, 'head')
- grad_b_query: float32 [2048], P('head')
- grad_b_value: float32 [2048], P('head')
- output_weight_gradient: float32 [2048, 2048], P('head')
- grad_b_out: float32 [2048], replicated
- grad_gain_one: float32 [2048], replicated
- grad_shift_one: float32 [2048], replicated
- grad_gain_two: float32 [2048], replicated
- grad_shift_two: float32 [2048], replicated
- grad_w_up: float32 [2048, 8192], P('head', 'seq')
- grad_b_up: float32 [8192], replicated
- grad_w_down: float32 [8192, 2048], P('seq', 'head')
- grad_b_down: float32 [2048], replicated
Inputs may be any that keep to these rules, and one draw needn't show every extreme that they name: counts[s, 0] is how many of the 50 earlier summary states of segment s are used, counts[s, 1] how many of its own 50 summary slots; the first ones in both cases.
All inputs are finite; a program needn't handle non-finite values.
Results may differ from a plain program's by a relative error of at most 0.025.
Values may be sent and summed in bfloat16 or wider, within the bound.
A program may use at most 384 MiB of HBM per device.

v0:
```python
import jax
import jax.numpy as jnp
from jax import lax
from jax.sharding import PartitionSpec as P

HDIM = 64


EPSILON = 1e-05
NEGATIVE = -1e30
LOWTYPE = jnp.bfloat16
WIDE_NUMBER_TYPE = jnp.float32


def layer_norm(values, gain_vec, shift_vec):
    row_mean = jnp.mean(values, axis=-1, keepdims=True)
    centered = values - row_mean
    row_var = jnp.mean(centered * centered, axis=-1, keepdims=True)
    return centered * lax.rsqrt(row_var + EPSILON) * gain_vec + shift_vec


def norm_back(values, gain_vec, shift_vec, incoming):
    unused, pullback = jax.vjp(layer_norm, values, gain_vec, shift_vec)
    return pullback(incoming)


def gelu_back(preactivation_hidden, incoming):
    unused, pullback = jax.vjp(
        lambda inner_act: jax.nn.gelu(inner_act, approximate=True), preactivation_hidden
    )
    return pullback(incoming)[0]


def head_sum(up_contribution, down_contribution):
    return (
        lax.psum_scatter(
            up_contribution.astype(jnp.bfloat16), "head", scatter_dimension=0, tiled=True
        ).astype(jnp.float32),
        lax.psum_scatter(
            down_contribution.astype(jnp.bfloat16), "head", scatter_dimension=0, tiled=True
        ).astype(jnp.float32),
    )


def key_allowed(count_row, row_start, block_rows, slot_count, length):
    query_pos = row_start + jnp.arange(block_rows, dtype=jnp.int32)
    key_pos = jnp.arange(slot_count + length, dtype=jnp.int32) - slot_count
    text_rows = length - slot_count
    memory_ok = (key_pos < 0) & (key_pos + slot_count < count_row[0])
    own_ok = (key_pos >= 0) & ((key_pos < text_rows) | (key_pos - text_rows < count_row[1]))
    return (memory_ok | own_ok)[None, :] & (key_pos[None, :] <= query_pos[:, None])


def block_scores(query_block, key_block, factor):
    return (
        jnp.einsum("qhe,khe->hqk", query_block, key_block, preferred_element_type=WIDE_NUMBER_TYPE)
        * factor
    )


def on_device(
    hidden,
    memory,
    counts,
    w_qkv,
    b_query,
    b_value,
    output_weight,
    b_out,
    gain_one,
    shift_one,
    gain_two,
    shift_two,
    w_up,
    up_bias,
    w_down,
    b_down,
    cotangent,
):
    hidden_full = hidden.astype(WIDE_NUMBER_TYPE)
    memory_full = memory.astype(WIDE_NUMBER_TYPE)
    normed = layer_norm(hidden_full, gain_one, shift_one).astype(LOWTYPE)
    mem_normed = layer_norm(memory_full, gain_one, shift_one).astype(LOWTYPE)
    gathered = lax.all_gather(normed, "head", axis=0, tiled=True)
    length = gathered.shape[0]
    seq_count = gathered.shape[1]
    slot_count = memory.shape[0]
    width = w_qkv.shape[2]
    head_count = width // HDIM
    key_count = slot_count + length
    block_rows = min(512, length)
    block_count = length // block_rows
    factor = HDIM ** (-0.5)
    biases = jnp.stack([b_query, jnp.zeros_like(b_query), b_value])
    projected = (
        jnp.einsum("lsd,dcf->lscf", gathered, w_qkv, preferred_element_type=WIDE_NUMBER_TYPE)
        + biases
    ).astype(LOWTYPE)
    mem_projected = (
        jnp.einsum(
            "nsd,dcf->nscf", mem_normed, w_qkv[:, 1:], preferred_element_type=WIDE_NUMBER_TYPE
        )
        + biases[1:]
    ).astype(LOWTYPE)
    queries = jnp.transpose(projected[:, :, 0], (1, 0, 2))
    key_rows = jnp.transpose(
        jnp.concatenate([mem_projected[:, :, 0], projected[:, :, 1]], axis=0), (1, 0, 2)
    )
    value_rows = jnp.transpose(
        jnp.concatenate([mem_projected[:, :, 1], projected[:, :, 2]], axis=0), (1, 0, 2)
    )

    def block_inputs(item_index):
        seq_index = item_index // block_count
        row_start = item_index % block_count * block_rows
        query_block = lax.dynamic_slice(queries, (seq_index, row_start, 0), (1, block_rows, width))[
            0
        ]
        query_block = query_block.reshape(block_rows, head_count, HDIM)
        key_block = lax.dynamic_index_in_dim(key_rows, seq_index, 0, keepdims=False).reshape(
            key_count, head_count, HDIM
        )
        value_block = lax.dynamic_index_in_dim(value_rows, seq_index, 0, keepdims=False).reshape(
            key_count, head_count, HDIM
        )
        count_row = lax.dynamic_index_in_dim(counts, seq_index, 0, keepdims=False)
        allowed = key_allowed(count_row, row_start, block_rows, slot_count, length)[None]
        return (seq_index, row_start, query_block, key_block, value_block, allowed)

    def forward_item(item_index):
        seq_index, row_start, query_block, key_block, value_block, allowed = block_inputs(
            item_index
        )
        scores = jnp.where(allowed, block_scores(query_block, key_block, factor), NEGATIVE)
        row_peak = jnp.max(scores, axis=-1, keepdims=True)
        raised = jnp.exp(scores - row_peak)
        row_total = jnp.sum(raised, axis=-1, keepdims=True)
        weights = (raised / row_total).astype(LOWTYPE)
        attended = jnp.einsum(
            "hqk,khe->qhe", weights, value_block, preferred_element_type=WIDE_NUMBER_TYPE
        )
        return (
            attended.astype(LOWTYPE).reshape(block_rows, width),
            row_peak[..., 0] + jnp.log(row_total[..., 0]),
        )

    items = jnp.arange(seq_count * block_count, dtype=jnp.int32)
    attn_blocks, log_sums = lax.map(forward_item, items)
    attention_result = jnp.transpose(attn_blocks.reshape(seq_count, length, width), (1, 0, 2))
    partial_rows = attention_result
    attn_out = lax.psum_scatter(
        jnp.einsum(
            "wpy,yo->wpo", partial_rows, output_weight, preferred_element_type=WIDE_NUMBER_TYPE
        ).astype(jnp.bfloat16),
        "head",
        scatter_dimension=0,
        tiled=True,
    ).astype(jnp.float32)
    resid = hidden_full + attn_out + b_out
    second_normed_rows = layer_norm(resid, gain_two, shift_two).astype(LOWTYPE)
    wide_up_product, wide_down_product = (
        lax.all_gather(w_up, "seq", axis=1, tiled=True),
        lax.all_gather(w_down, "seq", axis=0, tiled=True),
    )
    preactivation_hidden = (
        jnp.einsum(
            "mhj,ju->mhu",
            second_normed_rows,
            wide_up_product,
            preferred_element_type=WIDE_NUMBER_TYPE,
        )
        + up_bias
    )
    activated_hidden = jax.nn.gelu(preactivation_hidden, approximate=True).astype(LOWTYPE)
    branch_output = jnp.einsum(
        "wpy,yo->wpo", activated_hidden, wide_down_product, preferred_element_type=WIDE_NUMBER_TYPE
    )
    output = (resid + branch_output + b_down).astype(LOWTYPE)
    cot_full = cotangent.astype(WIDE_NUMBER_TYPE)
    activation_gradient = jnp.einsum(
        "zwb,ab->zwa", cotangent, wide_down_product, preferred_element_type=WIDE_NUMBER_TYPE
    )
    grad_pre = gelu_back(preactivation_hidden, activation_gradient)
    grad_b_up = jnp.sum(grad_pre, axis=(0, 1))
    preactivation_gradient_narrow = grad_pre.astype(LOWTYPE)
    grad_normed_two = jnp.einsum(
        "vxh,zh->vxz",
        preactivation_gradient_narrow,
        wide_up_product,
        preferred_element_type=WIDE_NUMBER_TYPE,
    )
    up_contribution = jnp.einsum(
        "rjy,rjx->yx",
        second_normed_rows,
        preactivation_gradient_narrow,
        preferred_element_type=WIDE_NUMBER_TYPE,
    )
    down_contribution = jnp.einsum(
        "rjy,rjx->yx", cotangent, activated_hidden, preferred_element_type=WIDE_NUMBER_TYPE
    )
    part_up, part_down = head_sum(up_contribution, down_contribution)
    grad_w_up, grad_down_cols = (
        lax.psum_scatter(
            part_up.astype(jnp.bfloat16), "seq", scatter_dimension=1, tiled=True
        ).astype(jnp.float32),
        lax.psum_scatter(
            part_down.astype(jnp.bfloat16), "seq", scatter_dimension=1, tiled=True
        ).astype(jnp.float32),
    )
    grad_w_down = jnp.transpose(grad_down_cols)
    grad_resid_norm, grad_gain_two, grad_shift_two = norm_back(
        resid, gain_two, shift_two, grad_normed_two
    )
    grad_resid = cot_full + grad_resid_norm
    grad_b_out = jnp.sum(grad_resid, axis=(0, 1))
    grad_b_down = jnp.sum(cot_full, axis=(0, 1))
    residual_rows_total = lax.all_gather(grad_resid.astype(LOWTYPE), "head", axis=0, tiled=True)
    grad_attention = jnp.einsum(
        "zwb,ab->zwa", residual_rows_total, output_weight, preferred_element_type=WIDE_NUMBER_TYPE
    ).astype(LOWTYPE)
    output_weight_gradient = jnp.einsum(
        "ncr,ncu->ru",
        attention_result,
        residual_rows_total,
        preferred_element_type=WIDE_NUMBER_TYPE,
    )
    grad_attn_seq = jnp.transpose(grad_attention, (1, 0, 2))

    def backward_item(item_index):
        seq_index, row_start, query_block, key_block, value_block, allowed = block_inputs(
            item_index
        )
        row_lse = lax.dynamic_index_in_dim(log_sums, item_index, 0, keepdims=False)
        scores = block_scores(query_block, key_block, factor)
        weights = jnp.where(allowed, jnp.exp(scores - row_lse[..., None]), 0.0)
        grad_block = lax.dynamic_slice(
            grad_attn_seq, (seq_index, row_start, 0), (1, block_rows, width)
        )[0]
        grad_block = grad_block.reshape(block_rows, head_count, HDIM)
        grad_weights = jnp.einsum(
            "qhe,khe->hqk", grad_block, value_block, preferred_element_type=WIDE_NUMBER_TYPE
        )
        inner_sum = jnp.sum(grad_weights * weights, axis=-1, keepdims=True)
        grad_scores = (weights * (grad_weights - inner_sum)).astype(LOWTYPE)
        grad_query = (
            jnp.einsum(
                "hqk,khe->qhe", grad_scores, key_block, preferred_element_type=WIDE_NUMBER_TYPE
            )
            * factor
        ).astype(LOWTYPE)
        grad_keys = (
            jnp.einsum(
                "hqk,qhe->khe", grad_scores, query_block, preferred_element_type=WIDE_NUMBER_TYPE
            )
            * factor
        )
        grad_values = jnp.einsum(
            "hqk,qhe->khe",
            weights.astype(LOWTYPE),
            grad_block,
            preferred_element_type=WIDE_NUMBER_TYPE,
        )
        return (
            grad_query.reshape(block_rows, width),
            grad_keys.reshape(key_count, width),
            grad_values.reshape(key_count, width),
        )

    grad_q_blocks, grad_k_blocks, grad_v_blocks = lax.map(backward_item, items)
    grad_q_seq = grad_q_blocks.reshape(seq_count, length, width)
    grad_k_seq = jnp.sum(
        grad_k_blocks.reshape(seq_count, block_count, key_count, width), axis=1
    ).astype(LOWTYPE)
    grad_v_seq = jnp.sum(
        grad_v_blocks.reshape(seq_count, block_count, key_count, width), axis=1
    ).astype(LOWTYPE)
    grad_own = jnp.transpose(
        jnp.stack([grad_q_seq, grad_k_seq[:, slot_count:], grad_v_seq[:, slot_count:]], axis=2),
        (1, 0, 2, 3),
    )
    grad_mem = jnp.transpose(
        jnp.stack([grad_k_seq[:, :slot_count], grad_v_seq[:, :slot_count]], axis=2), (1, 0, 2, 3)
    )
    grad_b_query = jnp.sum(grad_q_seq.astype(WIDE_NUMBER_TYPE), axis=(0, 1))
    grad_b_value = jnp.sum(grad_v_seq.astype(WIDE_NUMBER_TYPE), axis=(0, 1))
    grad_w_qkv = jnp.einsum(
        "lsd,lscf->dcf", gathered, grad_own, preferred_element_type=WIDE_NUMBER_TYPE
    )
    grad_w_mem = jnp.einsum(
        "nsd,nscf->dcf", mem_normed, grad_mem, preferred_element_type=WIDE_NUMBER_TYPE
    )
    grad_w_qkv = grad_w_qkv + jnp.concatenate(
        [jnp.zeros_like(grad_w_mem[:, :1]), grad_w_mem], axis=1
    )
    partial_rows = grad_own
    grad_normed = lax.psum_scatter(
        jnp.einsum(
            "lscf,dcf->lsd", partial_rows, w_qkv, preferred_element_type=WIDE_NUMBER_TYPE
        ).astype(jnp.bfloat16),
        "head",
        scatter_dimension=0,
        tiled=True,
    ).astype(jnp.float32)
    grad_mem_normed = jnp.einsum(
        "nscf,dcf->nsd", grad_mem, w_qkv[:, 1:], preferred_element_type=WIDE_NUMBER_TYPE
    )
    grad_hidden_norm, gain_rows, shift_rows = norm_back(
        hidden_full, gain_one, shift_one, grad_normed
    )
    grad_mem_part, gain_states, shift_states = norm_back(
        memory_full, gain_one, shift_one, grad_mem_normed
    )
    grad_memory = lax.psum(grad_mem_part.astype(jnp.bfloat16), "head").astype(jnp.float32)
    grad_hidden = grad_resid + grad_hidden_norm
    grad_w_qkv, grad_b_query, grad_b_value, output_weight_gradient = (
        lax.psum(grad_w_qkv.astype(jnp.bfloat16), "seq").astype(jnp.float32),
        lax.psum(grad_b_query.astype(jnp.bfloat16), "seq").astype(jnp.float32),
        lax.psum(grad_b_value.astype(jnp.bfloat16), "seq").astype(jnp.float32),
        lax.psum(output_weight_gradient.astype(jnp.bfloat16), "seq").astype(jnp.float32),
    )
    totals = lax.psum(
        (
            grad_b_out,
            grad_b_up,
            grad_b_down,
            gain_rows + gain_states,
            shift_rows + shift_states,
            grad_gain_two,
            grad_shift_two,
        ),
        ("head", "seq"),
    )
    return (
        output,
        grad_hidden,
        grad_memory,
        grad_w_qkv,
        grad_b_query,
        grad_b_value,
        output_weight_gradient,
        totals[0],
        totals[3],
        totals[4],
        totals[5],
        totals[6],
        grad_w_up,
        totals[1],
        grad_w_down,
        totals[2],
    )


def solution(mesh):
    return jax.shard_map(
        on_device,
        mesh=mesh,
        in_specs=(
            P("head", "seq", None),
            P(None, "seq", None),
            P("seq", None),
            P(None, None, "head"),
            P("head"),
            P("head"),
            P("head", None),
            P(),
            P(),
            P(),
            P(),
            P(),
            P(None, "seq"),
            P(),
            P("seq", None),
            P(),
            P("head", "seq", None),
        ),
        out_specs=(
            P("head", "seq", None),
            P("head", "seq", None),
            P(None, "seq", None),
            P(None, None, "head"),
            P("head"),
            P("head"),
            P("head", None),
            P(),
            P(),
            P(),
            P(),
            P(),
            P("head", "seq"),
            P(),
            P("seq", "head"),
            P(),
        ),
        check_vma=False,
    )
```

profile of v0, /device:TPU:1, one launch (start us, length us, event | category | flops | bytes accessed | tf_op | source)
XLA Modules:
  0.0 2637.6 jit_solution(11064316743649035740)
XLA Ops:
  18.6 71.5 %all-gather.5.cloned.1.call-done = bf16[2048,1,2048]{2,0,1:T(8,128)(2,1)} async-done(((bf16[128,1,2048]{2,0,1:T(8,128)(2,1)}), bf16[2048,1,2048]{2,0,1:T(8,128)(2,1)}) %all-gather.5.cloned.1.call-update) | async-done | bytes 8388624 | tf_op jit(solution)/shard_map/all_gather | solution.py:84
  90.1 7.9 fusion.40
  99.3 54.0 %while.34 = (s32[]{:T(128)}, bf16[4,512,128]{2,1,0:T(8,128)(2,1)}, f32[4,2,512]{2,1,0:T(2,128)S(1)}, s32[1,2]{1,0:T(1,128)S(1)}, s32[4]{0:T(128)S(1)}, /*index=5...) while((s32[]{:T(128)}, bf16[4,512,128]{2,1,0:T(8,128)(2,1)}, ...), condition=%wide.region_7.8_spmd, body=%wide.region_4.7_spmd.sunk | while | flops 577996928 | bytes 32257872 | solution.py:148
  153.3 6.6 convert_bitcast_fusion.1
  161.1 361.2 %reduce-scatter.9.cloned.1.call-done = bf16[128,1,2048]{2,0,1:T(8,128)(2,1)} async-done(((bf16[2048,1,2048]{2,0,1:T(8,128)(2,1)}), bf16[128,1,2048]{2,0,1:T(8,128)(2,1)}) %reduce-scatter.9.cloned.1.call-update) | async-done | bytes 524304 | tf_op jit(solution)/shard_map/reduce_scatter | solution.py:151
  525.0 302.6 %all-gather.7.cloned.1.call-done = bf16[2048,8192]{1,0:T(8,128)(2,1)} async-done(((bf16[2048,1024]{1,0:T(8,128)(2,1)}), bf16[2048,8192]{1,0:T(8,128)(2,1)}) %all-gather.7.cloned.1.call-update) | async-done | bytes 33554448 | tf_op jit(solution)/shard_map/all_gather | solution.py:162
  827.6 17.5 convolution_add_fusion
  845.1 625.3 %all-gather.9.cloned.1.call-done = bf16[8192,2048]{1,0:T(8,128)(2,1)} async-done(((bf16[1024,2048]{1,0:T(8,128)(2,1)}), bf16[8192,2048]{1,0:T(8,128)(2,1)}) %all-gather.9.cloned.1.call-update) | async-done | bytes 33554448 | tf_op jit(solution)/shard_map/all_gather | solution.py:163
  1470.4 20.2 fusion.117
  1490.5 19.6 fusion.69
  1514.9 16.2 convert_bitcast_fusion
  1531.1 40.7 %copy.72 = bf16[2048,8192]{1,0:T(8,128)(2,1)} copy(bf16[2048,8192]{0,1:T(8,128)(2,1)} %convert_bitcast_fusion) | data formatting | bytes 67108864
  1571.9 15.7 convolution_convert_fusion
  1589.2 5.7 fusion.52
  1595.0 171.5 %while.35 = (s32[]{:T(128)}, bf16[4,512,128]{1,2,0:T(8,128)(2,1)}, f32[4,2098,128]{1,2,0:T(8,128)}, f32[4,2098,128]{1,2,0:T(8,128)}, s32[1,2]{1,0:T(1,128)S(1)},...) while((s32[]{:T(128)}, bf16[4,512,128]{1,2,0:T(8,128)(2,1)}, ...), condition=%wide.region_15.16_spmd, body=%wide.region_13.15_spmd.sunk | while | flops 1396853120 | bytes 93467256 | solution.py:269
  1602.9 5.6 exponential_select_fusion.2
  1608.7 10.8 multiply_reduce_fusion.3
  1619.5 11.4 multiply_convert_fusion.5
  1633.5 6.3 fusion.185
  1651.7 4.8 exponential_select_fusion.2
  1656.7 8.1 multiply_reduce_fusion.3
  1664.7 8.3 multiply_convert_fusion.5
  1675.7 5.3 fusion.185
  1692.6 4.8 exponential_select_fusion.2
  1697.5 8.2 multiply_reduce_fusion.3
  1705.7 8.6 multiply_convert_fusion.5
  1716.9 4.9 fusion.185
  1733.4 4.8 exponential_select_fusion.2
  1738.4 8.4 multiply_reduce_fusion.3
  1746.8 8.5 multiply_convert_fusion.5
  1757.9 4.8 fusion.185
  1766.5 2.6 reduce_sum.284
  1769.4 2.6 reduce_sum.283
  1778.2 5.6 fusion.48
  1783.8 7.1 fusion.27
  1792.9 10.0 fusion.31
  1803.1 32.5 %reduce-scatter.19.cloned.1.call-done = bf16[128,8192]{1,0:T(8,128)(2,1)} async-done(((bf16[2048,8192]{1,0:T(8,128)(2,1)}), bf16[128,8192]{1,0:T(8,128)(2,1)}) %reduce-scatter.19.cloned.1.call-update) | async-done | bytes 2097168
  1835.5 4.1 copy.73
  1839.7 247.0 %reduce-scatter.13.cloned.1.call-done = bf16[128,8192]{1,0:T(8,128)(2,1)} async-done(((bf16[2048,8192]{1,0:T(8,128)(2,1)}), bf16[128,8192]{1,0:T(8,128)(2,1)}) %reduce-scatter.13.cloned.1.call-update) | async-done | bytes 2097168 | tf_op jit(solution)/shard_map/reduce_scatter | solution.py:36
  2087.7 17.9 fusion.51
  2106.1 16.9 all-reduce.3
  2124.0 102.0 %all-reduce.9.cloned.1.call-done = bf16[50,1,2048]{2,0,1:T(8,128)(2,1)} async-done(((bf16[50,1,2048]{2,0,1:T(8,128)(2,1)}), bf16[50,1,2048]{2,0,1:T(8,128)(2,1)}) %all-reduce.9.cloned.1.call-update) | async-done | bytes 204816 | tf_op jit(solution)/shard_map/psum | solution.py:313
  2228.0 106.9 %all-reduce.13.cloned.1.call-done = (bf16[2048,3,128]{2,0,1:T(8,128)(2,1)}, bf16[128,2048]{1,0:T(8,128)(2,1)}) async-done(((bf16[2048,3,128]{2,0,1:T(8,128)(2,1)}, bf16[128,2048]{1,0:T(8,128)(2,1)}), (bf16[2048,3,128]{2,0,1:T(8,128)(2,1)}, bf16[128,2048]{1,0:T(8,128)(2,1)})) %all-reduce.13.cloned.1.call-update) | async-done | bytes 2097168 | tf_op jit(solution)/shard_map/psum | solution.py:316
  2334.9 3.4 convert_element_type.219
  2339.4 101.1 %reduce-scatter.11.cloned.1.call-done = bf16[128,1,2048]{2,0,1:T(8,128)(2,1)} async-done(((bf16[2048,1,2048]{2,0,1:T(8,128)(2,1)}), bf16[128,1,2048]{2,0,1:T(8,128)(2,1)}) %reduce-scatter.11.cloned.1.call-update) | async-done | bytes 524304 | tf_op jit(solution)/shard_map/reduce_scatter | solution.py:296
  2449.4 46.0 %reduce-scatter.17.cloned.1.call-done = bf16[128,1024]{0,1:T(8,128)(2,1)} async-done(((bf16[128,8192]{0,1:T(8,128)(2,1)}), bf16[128,1024]{0,1:T(8,128)(2,1)}) %reduce-scatter.17.cloned.1.call-update) | async-done | bytes 262160 | tf_op jit(solution)/shard_map/reduce_scatter | solution.py:206
  2497.1 53.2 %reduce-scatter.15.cloned.1.call-done = bf16[128,1024]{1,0:T(8,128)(2,1)} async-done(((bf16[128,8192]{1,0:T(8,128)(2,1)}), bf16[128,1024]{1,0:T(8,128)(2,1)}) %reduce-scatter.15.cloned.1.call-update) | async-done | bytes 262160 | tf_op jit(solution)/shard_map/reduce_scatter | solution.py:203
  2552.1 68.4 %all-reduce.11.cloned.1.call-done = (f32[2048]{0:T(1024)}, f32[2048]{0:T(1024)}, f32[2048]{0:T(1024)}, f32[2048]{0:T(1024)}, f32[2048]{0:T(1024)}, /*index=5*/f32[8192]{0:T(1024)}, f32[2048]{0:T(1024)}) async-done(((f32[2048]{0:T(1024)}, f32[2048]{0:T(1024)}, f32[2048]{0:T(1024)}, f32[2048]{0:T(1024)}, f32[2048]{0:T(1024)}, /*index=5*/f32[8192]{0:T(1024)}, f32[2048]{0:T(1024)}), (f32[2048]{0:T(1024)}, ...) | async-done | bytes 81936 | tf_op jit(solution)/shard_map/psum | solution.py:321
  (363 shorter events, 146.7 us)
Async XLA Ops:
  8.0 145.2 %copy-start = (bf16[128,2048]{1,0:T(8,128)(2,1)S(1)}, bf16[128,2048]{1,0:T(8,128)(2,1)}, u32[]{:S(2)}) copy-start(bf16[128,2048]{1,0:T(8,128)(2,1)} %param.27) | copy-start | bytes 1572868
  8.0 82.0 %copy-start.52 = (bf16[2048,3,128]{2,0,1:T(8,128)(2,1)S(1)}, bf16[2048,3,128]{2,0,1:T(8,128)(2,1)}, u32[]{:S(2)}) copy-start(bf16[2048,3,128]{2,0,1:T(8,128)(2,1)} %param.24) | copy-start | bytes 4718596
  8.1 82.0 %all-gather.5.cloned.1.call-start = ((), (), s32[]{:S(2)}) async-start(), calls=%async_computation.6 | async-start | bytes 8912896 | tf_op jit(solution)/shard_map/all_gather | solution.py:84
  13.6 508.7 %reduce-scatter.9.cloned.1.call-start = ((), (), s32[]{:S(2)}) async-start(), calls=%async_computation.7 | async-start | bytes 8912896 | tf_op jit(solution)/shard_map/reduce_scatter | solution.py:151
  15.5 82.5 %copy-start.40 = (f32[50]{0:T(128)}, f32[50]{0:T(128)S(1)}, u32[]{:S(2)}) copy-start(f32[50]{0:T(128)S(1)} %broadcast_multiply_fusion) | copy-start | bytes 604
  16.7 81.3 %copy-start.47 = (f32[50]{0:T(128)}, f32[50]{0:T(128)S(1)}, u32[]{:S(2)}) copy-start(f32[50]{0:T(128)S(1)} %fusion.95) | copy-start | bytes 604
  16.7 81.3 %copy-start.42 = (f32[50]{0:T(128)}, f32[50]{0:T(128)S(1)}, u32[]{:S(2)}) copy-start(f32[50]{0:T(128)S(1)} %fusion.99) | copy-start | bytes 604
  159.8 362.5 %copy-start.2 = (bf16[128,1,2048]{2,0,1:T(8,128)(2,1)S(1)}, bf16[128,1,2048]{2,0,1:T(8,128)(2,1)}, u32[]{:S(2)}) copy-start(bf16[128,1,2048]{2,0,1:T(8,128)(2,1)} %param.21) | copy-start | bytes 1572868
  159.9 362.5 %copy-start.23 = (f32[2048]{0:T(1024)S(1)}, f32[2048]{0:T(1024)}, u32[]{:S(2)}) copy-start(f32[2048]{0:T(1024)} %param.28) | copy-start | bytes 24580
  159.9 667.8 %all-gather.7.cloned.1.call-start = ((), (), s32[]{:S(2)}) async-start(), calls=%async_computation.8 | async-start | bytes 37748736 | tf_op jit(solution)/shard_map/all_gather | solution.py:162
  160.4 667.2 %copy-start.30 = (f32[2048]{0:T(1024)S(1)}, f32[2048]{0:T(1024)}, u32[]{:S(2)}) copy-start(f32[2048]{0:T(1024)} %param.31) | copy-start | bytes 24580
  160.5 667.2 %copy-start.33 = (f32[2048]{0:T(1024)S(1)}, f32[2048]{0:T(1024)}, u32[]{:S(2)}) copy-start(f32[2048]{0:T(1024)} %param.32) | copy-start | bytes 24580
  160.5 667.2 %copy-start.35 = (f32[8192]{0:T(1024)S(1)}, f32[8192]{0:T(1024)}, u32[]{:S(2)}) copy-start(f32[8192]{0:T(1024)} %param.34) | copy-start | bytes 98308
  160.5 1309.9 %all-gather.9.cloned.1.call-start = ((), (), s32[]{:S(2)}) async-start(), calls=%async_computation.9 | async-start | bytes 37748736 | tf_op jit(solution)/shard_map/all_gather | solution.py:163
  161.1 1428.2 %all-gather.11.cloned.1.call-start = ((), (), s32[]{:S(2)}) async-start(), calls=%async_computation.10 | async-start | bytes 8912896 | tf_op jit(solution)/shard_map/all_gather | solution.py:217
  845.1 645.4 %copy-start.8 = (bf16[128,1,2048]{2,0,1:T(8,128)(2,1)S(1)}, bf16[128,1,2048]{2,0,1:T(8,128)(2,1)}, u32[]{:S(2)}) copy-start(bf16[128,1,2048]{2,0,1:T(8,128)(2,1)} %reduce-scatter.9.cloned.1.call-done) | copy-start | bytes 1572868
  1511.8 19.3 copy-start.44
  1514.8 320.7 %reduce-scatter.19.cloned.1.call-start = ((), (), s32[]{:S(2)}) async-start(), calls=%async_computation.16 | async-start | bytes 35651584
  1571.8 514.9 %reduce-scatter.13.cloned.1.call-start = ((), (), s32[]{:S(2)}) async-start(), calls=%async_computation.13 | async-start | bytes 35651584 | tf_op jit(solution)/shard_map/reduce_scatter | solution.py:36
  1587.6 638.4 %all-reduce.9.cloned.1.call-start = ((), (), s32[]{:S(2)}) async-start(), calls=%async_computation.12 | async-start | bytes 458752 | tf_op jit(solution)/shard_map/psum | solution.py:313
  1595.0 13.5 copy-start.4
  1595.0 13.5 copy-start.13
  1595.0 13.5 copy-start.21
  1595.0 13.7 copy-start.6
  1643.8 12.6 copy-start.4
  1643.8 12.6 copy-start.13
  1643.9 12.6 copy-start.21
  1643.9 12.8 copy-start.6
  1684.7 12.8 copy-start.6
  1725.6 12.8 copy-start.6
  1778.1 556.8 %all-reduce.13.cloned.1.call-start = ((), (), s32[]{:S(2)}) async-start(), calls=%async_computation.18 | async-start | bytes 4194304 | tf_op jit(solution)/shard_map/psum | solution.py:316
  1792.9 647.7 %reduce-scatter.11.cloned.1.call-start = ((), (), s32[]{:S(2)}) async-start(), calls=%async_computation.11 | async-start | bytes 8912896 | tf_op jit(solution)/shard_map/reduce_scatter | solution.py:296
  1803.0 284.1 %copy-start.12 = (f32[128,2048]{1,0:T(8,128)S(1)}, f32[128,2048]{1,0:T(8,128)}, u32[]{:S(2)}) copy-start(f32[128,2048]{1,0:T(8,128)} %get-tuple-element.593) | copy-start | bytes 3145732
  1803.0 284.7 %copy-start.3 = (bf16[128,1,2048]{2,0,1:T(8,128)(2,1)S(1)}, bf16[128,1,2048]{2,0,1:T(8,128)(2,1)}, u32[]{:S(2)}) copy-start(bf16[128,1,2048]{2,0,1:T(8,128)(2,1)} %param.21) | copy-start | bytes 1572868
  1803.0 284.7 %copy-start.9 = (bf16[128,1,2048]{2,0,1:T(8,128)(2,1)S(1)}, bf16[128,1,2048]{2,0,1:T(8,128)(2,1)}, u32[]{:S(2)}) copy-start(bf16[128,1,2048]{2,0,1:T(8,128)(2,1)} %reduce-scatter.9.cloned.1.call-done) | copy-start | bytes 1572868
  1803.0 284.7 %copy-start.24 = (f32[2048]{0:T(1024)S(1)}, f32[2048]{0:T(1024)}, u32[]{:S(2)}) copy-start(f32[2048]{0:T(1024)} %param.28) | copy-start | bytes 24580
  1803.0 284.7 %copy-start.53 = (f32[2048]{0:T(1024)S(1)}, f32[2048]{0:T(1024)}, u32[]{:S(2)}) copy-start(f32[2048]{0:T(1024)} %param.36) | copy-start | bytes 24580
  1803.0 692.3 %reduce-scatter.17.cloned.1.call-start = ((), (), s32[]{:S(2)}) async-start(), calls=%async_computation.15 | async-start | bytes 2359296 | tf_op jit(solution)/shard_map/reduce_scatter | solution.py:206
  1839.6 710.7 %reduce-scatter.15.cloned.1.call-start = ((), (), s32[]{:S(2)}) async-start(), calls=%async_computation.14 | async-start | bytes 2359296 | tf_op jit(solution)/shard_map/reduce_scatter | solution.py:203
  2086.7 533.7 %all-reduce.11.cloned.1.call-start = ((), (), s32[]{:S(2)}) async-start(), calls=%async_computation.17 | async-start | bytes 163840 | tf_op jit(solution)/shard_map/psum | solution.py:321
  2087.7 36.3 %copy-start.20 = (f32[50,2048,1]{1,0,2:T(8,128)S(1)}, f32[50,2048,1]{1,0,2:T(8,128)}, u32[]{:S(2)}) copy-start(f32[50,2048,1]{1,0,2:T(8,128)} %copy-done.19) | copy-start | bytes 1228804
  2105.6 334.9 %copy-start.37 = (f32[128]{0:T(128)S(1)}, f32[128]{0:T(128)}, u32[]{:S(2)}) copy-start(f32[128]{0:T(128)} %copy-done.36) | copy-start | bytes 1540
  2124.0 318.0 %copy-start.51 = (f32[128]{0:T(128)S(1)}, f32[128]{0:T(128)}, u32[]{:S(2)}) copy-start(f32[128]{0:T(128)} %copy-done.50) | copy-start | bytes 1540
  2124.0 318.0 %copy-start.39 = (f32[128]{0:T(128)S(1)}, f32[128]{0:T(128)}, u32[]{:S(2)}) copy-start(f32[128]{0:T(128)} %copy-done.38) | copy-start | bytes 1540
  2334.9 108.8 %copy-start.11 = (f32[128,1,2048]{2,0,1:T(8,128)S(1)}, f32[128,1,2048]{2,0,1:T(8,128)}, u32[]{:S(2)}) copy-start(f32[128,1,2048]{2,0,1:T(8,128)} %copy-done.10) | copy-start | bytes 3145732
  2334.9 108.8 %copy-start.16 = (bf16[128,1,2048]{2,0,1:T(8,128)(2,1)S(1)}, bf16[128,1,2048]{2,0,1:T(8,128)(2,1)}, u32[]{:S(2)}) copy-start(bf16[128,1,2048]{2,0,1:T(8,128)(2,1)} %param.37) | copy-start | bytes 1572868
  2334.9 108.8 %copy-start.45 = (f32[128]{0:T(128)S(1)}, f32[128]{0:T(128)}, u32[]{:S(2)}) copy-start(f32[128]{0:T(128)} %copy-done.44) | copy-start | bytes 1540
  2442.0 187.6 %copy-start.1 = (bf16[128,2048]{1,0:T(8,128)(2,1)S(1)}, bf16[128,2048]{1,0:T(8,128)(2,1)}, u32[]{:S(2)}) copy-start(bf16[128,2048]{1,0:T(8,128)(2,1)} %param.27) | copy-start | bytes 1572868
  (43 other events, 206.9 us)
Sparse Core Ops, SparseCore 0:
  13.7 76.2 all-gather.4
  160.0 362.2 reduce-scatter.8
  1514.9 74.2 all-gather.10
  1593.5 241.9 reduce-scatter.18
  1840.5 246.1 reduce-scatter.12
  2089.6 136.3 all-reduce.8
  2229.9 104.9 all-reduce.12
  2339.9 100.6 reduce-scatter.10
  2443.0 52.3 reduce-scatter.16
  2497.6 52.6 reduce-scatter.14
Sparse Core Ops, SparseCore 1:
  162.0 665.6 all-gather.6
  829.1 641.2 all-gather.8
  2449.5 170.9 all-reduce.10
where the time goes:
time: 2650 us; the launch traced here: 2640 us
  waiting for transfers between devices  2120 us (80%)
  matrix products  263 us (10%)
  other arithmetic  105 us (4%)
  local copies, waits for them, and re-layouts  91.3 us (3%)
    all_gather x1, waiting for transfers between devices, on_device(): lax.all_gather(w_down, 'seq', axis=0, tiled=True)  625 us
    reduce_scatter x1, waiting for transfers between devices, on_device(): lax.psum_scatter(jnp.einsum('wpy,yo->wpo', partial_rows, output_weight, p...  361 us
    all_gather x1, waiting for transfers between devices, on_device(): lax.all_gather(w_up, 'seq', axis=1, tiled=True)  303 us
    reduce_scatter x1, waiting for transfers between devices, head_sum(): lax.psum_scatter(up_contribution.astype(jnp.bfloat16), 'head', scatter_di...  247 us
    psum x1, waiting for transfers between devices, on_device(): lax.psum(grad_w_qkv.astype(jnp.bfloat16), 'seq').astype(jnp.float32)  107 us
    psum x1, waiting for transfers between devices, on_device(): lax.psum(grad_mem_part.astype(jnp.bfloat16), 'head').astype(jnp.float32)  102 us
    reduce_scatter x1, waiting for transfers between devices, on_device(): lax.psum_scatter(jnp.einsum('lscf,dcf->lsd', partial_rows, w_qkv, preferr...  101 us
    all_gather x1, waiting for transfers between devices, on_device(): gathered = lax.all_gather(normed, 'head', axis=0, tiled=True)  71.5 us
  transfers between devices with their start and end apart: 13, of which 13 were waited for; matrix products, arithmetic and copies ran while one was open for 13% of the time, Pallas kernels for 0%

commit v1 on v0

v1 whole, which is shorter than its diff:
```python
import jax
import jax.numpy as jnp
from jax import lax
from jax.experimental import pallas as pl
from jax.experimental.pallas import tpu as pltpu
from jax.sharding import PartitionSpec as P

HDIM = 64
EPSILON = 1e-05
NEGATIVE = -1e30
LOW = jnp.bfloat16
WIDE = jnp.float32
QROWS = 256
KROWS = 512
MEMROWS = 64
BLOCK = 128
NEAR_FIRST = ((0, 0), (-1, 0), (1, 0), (0, 1), (2, 0), (-1, 1), (1, 1), (2, 1))
FAR_FIRST = ((2, 1), (2, 0), (1, 1), (-1, 1), (1, 0), (-1, 0), (0, 1), (0, 0))
MESH = pl.DeviceIdType.MESH
VMEM = pl.BlockSpec(memory_space=pltpu.VMEM)
ANY = pl.BlockSpec(memory_space=pl.ANY)
VMEM_LIMIT = 60 * 2**20


def dot(left, right):
    return jnp.dot(left, right, preferred_element_type=WIDE)


def dot_nt(left, right):
    return lax.dot_general(left, right, (((1,), (1,)), ((), ())), preferred_element_type=WIDE)


def dot_tn(left, right):
    return lax.dot_general(left, right, (((0,), (0,)), ((), ())), preferred_element_type=WIDE)


def row_tiles(rows, body, step=16):
    def run(i, carry):
        body(pl.ds(pl.multiple_of(i * step, step), step))
        return carry

    lax.fori_loop(0, rows // step, run, 0)


class Group:
    def __init__(self, axis):
        self.axis = axis
        index = lax.axis_index(axis)
        self.cores = 2 if axis == "head" else 1
        self.core = index % self.cores
        self.pair = index // self.cores % 2
        self.ring = index // (2 * self.cores)

    def chip(self, dr, dp):
        pair = 1 - self.pair if dp else self.pair
        return (self.ring + (dr + 4)) % 4 * 2 + pair

    def block(self, dr, dp, dc=0):
        core = 1 - self.core if dc else self.core
        return self.chip(dr, dp) * self.cores + core

    def device(self, dr, dp, dc=0):
        return {self.axis: self.block(dr, dp, dc)}

    def greet(self, barrier):
        peers = [(1, 0, 0), (-1, 0, 0), (0, 1, 0)] + ([(0, 0, 1)] if self.cores == 2 else [])
        for peer in peers:
            pl.semaphore_signal(barrier, 1, device_id=self.device(*peer), device_id_type=MESH)
        return len(peers)


def greet_all(*groups):
    barrier = pltpu.get_barrier_semaphore()
    pl.semaphore_wait(barrier, sum(group.greet(barrier) for group in groups))


class Gather:
    COPIES = 21

    def __init__(self, group, buf, send, recv, cut=BLOCK):
        self.group, self.buf, self.send, self.recv = group, buf, send, recv
        half = BLOCK // 2
        low = (cut // 2 + 15) // 16 * 16
        every, upper = (0, BLOCK), (cut, BLOCK - cut)
        ops = {
            "v0": ((0, 0), (1, 0, 0), every, (-1, 0)),
            "n0": ((0, 0), (-1, 0, 0), every, (1, 0)),
            "pair": ((0, 0), (0, 1, 0), every, (0, 1)),
            "v0h": ((-1, 0), (1, 0, 0), (0, half), (2, 0)),
            "n0h": ((1, 0), (-1, 0, 0), (half, half), (2, 0)),
            "v1": ((0, 1), (1, 0, 0), (0, cut), (-1, 1)),
            "n1": ((0, 1), (-1, 0, 0), (0, cut), (1, 1)),
            "v1h": ((-1, 1), (1, 0, 0), (0, low), (2, 1)),
            "n1h": ((1, 1), (-1, 0, 0), (low, cut - low), (2, 1)),
            "bv": ((-1, 0), (0, 1, 0), upper, (-1, 1)),
            "bn": ((1, 0), (0, 1, 0), upper, (1, 1)),
            "b2": ((2, 0), (0, 1, 0), upper, (2, 1)),
        }
        if group.cores == 2:
            for place in NEAR_FIRST:
                ops["s%d%d" % place] = (place, (0, 0, 1), every, place)
        self.ops = {name: (i,) + op for i, (name, op) in enumerate(ops.items()) if op[2][1] > 0}
        self.started = []
        self.inward = {
            (0, 0): (),
            (-1, 0): ("v0",),
            (1, 0): ("n0",),
            (0, 1): ("pair",),
            (2, 0): ("v0h", "n0h"),
            (-1, 1): ("v1", "bv"),
            (1, 1): ("n1", "bn"),
            (2, 1): ("v1h", "n1h", "b2"),
        }
        self.outward = {
            (0, 0): ("v0", "n0", "pair"),
            (-1, 0): ("v0h", "bv"),
            (1, 0): ("n0h", "bn"),
            (0, 1): ("v1", "n1"),
            (2, 0): ("b2",),
            (-1, 1): ("v1h",),
            (1, 1): ("n1h",),
            (2, 1): (),
        }

    def copy(self, name, arriving):
        i, place, peer, (start, count), source = self.ops[name]
        sibling = 1 if arriving and name[0] == "s" else 0
        block = self.group.block(*(source if arriving else place), sibling)
        view = self.buf.at[block] if count == BLOCK else self.buf.at[block, pl.ds(start, count)]
        return pltpu.make_async_remote_copy(
            src_ref=view,
            dst_ref=view,
            send_sem=self.send.at[i],
            recv_sem=self.recv.at[i],
            device_id=self.group.device(*peer),
            device_id_type=MESH,
        )

    def arrive(self, *place):
        for name in self.inward[place]:
            if name in self.ops:
                self.copy(name, True).wait_recv()
        names = self.outward[place]
        if self.group.cores == 2:
            names += ("s%d%d" % place,)
        for name in names:
            if name in self.ops:
                self.copy(name, False).start()
                self.started.append(name)

    def sibling(self, *place):
        if self.group.cores == 2:
            self.copy("s%d%d" % place, True).wait_recv()

    def drain(self):
        for name in self.started:
            self.copy(name, False).wait_send()


class Reduce:
    COPIES = 21

    def __init__(self, group, total, stage, land, send, recv, cut=BLOCK, near=None, result=None):
        self.group, self.total, self.land = group, total, land
        self.stage = total if stage is None else stage
        self.staged = stage is not None
        self.send, self.recv, self.near, self.result = send, recv, near, result
        half = BLOCK // 2
        low = (cut // 2 + 15) // 16 * 16
        every, upper = (0, BLOCK), (cut, BLOCK - cut)
        ops = {
            "b2": ((2, 1), (0, 1, 0), upper, 0),
            "n1h": ((2, 1), (1, 0, 0), (0, low), 1),
            "v1h": ((2, 1), (-1, 0, 0), (low, cut - low), 1),
            "n0h": ((2, 0), (1, 0, 0), (0, half), 2),
            "v0h": ((2, 0), (-1, 0, 0), (half, half), 2),
            "bn": ((1, 1), (0, 1, 0), upper, 3),
            "bv": ((-1, 1), (0, 1, 0), upper, 4),
            "n1": ((1, 1), (1, 0, 0), (0, cut), 3),
            "v1": ((-1, 1), (-1, 0, 0), (0, cut), 4),
            "n0": ((1, 0), (1, 0, 0), every, 5),
            "v0": ((-1, 0), (-1, 0, 0), every, 6),
            "pu": ((0, 1), (0, 1, 0), upper, 7),
            "pl": ((0, 1), (0, 1, 0), (0, cut), 7),
        }
        self.ops = {name: (i,) + op for i, (name, op) in enumerate(ops.items()) if op[2][1] > 0}
        self.cut = cut
        self.started = []
        self.early = {(1, 1): "bn", (-1, 1): "bv", (0, 1): "pu"}
        self.inward = {
            (2, 1): (),
            (2, 0): ("b2",),
            (1, 1): ("n1h",),
            (-1, 1): ("v1h",),
            (1, 0): ("bn", "n0h"),
            (-1, 0): ("bv", "v0h"),
            (0, 1): ("n1", "v1"),
            (0, 0): ("pu", "n0", "v0", "pl"),
        }
        self.outward = {
            (2, 1): ("b2", "n1h", "v1h"),
            (2, 0): ("n0h", "v0h"),
            (1, 1): ("n1",),
            (-1, 1): ("v1",),
            (1, 0): ("n0",),
            (-1, 0): ("v0",),
            (0, 1): ("pl",),
            (0, 0): (),
        }

    def copy(self, name):
        i, place, peer, (start, count), slot = self.ops[name]
        return pltpu.make_async_remote_copy(
            src_ref=self.stage.at[FAR_FIRST.index(place), pl.ds(start, count)],
            dst_ref=self.land.at[slot, pl.ds(start, count)],
            send_sem=self.send.at[i],
            recv_sem=self.recv.at[i],
            device_id=self.group.device(*peer),
            device_id_type=MESH,
        )

    def near_copy(self, k):
        return pltpu.make_async_remote_copy(
            src_ref=self.near[0].at[k],
            dst_ref=self.near[1].at[k],
            send_sem=self.send.at[13 + k],
            recv_sem=self.recv.at[13 + k],
            device_id=self.group.device(0, 0, 1),
            device_id_type=MESH,
        )

    def begin(self, name):
        self.copy(name).start()
        self.started.append(name)

    def blend(self, place, start, count, names):
        k = FAR_FIRST.index(place)
        spans = [self.ops[name][3] + (self.ops[name][4],) for name in names]
        marks = {start, start + count}
        for first, size, _ in spans:
            marks |= {m for m in (first, first + size) if start < m < start + count}
        marks = sorted(marks)
        for low, high in zip(marks, marks[1:]):
            slots = [slot for first, size, slot in spans if first <= low and high <= first + size]
            if not (slots or self.near or self.staged or place == (0, 0)):
                continue

            def body(rows):
                at = pl.ds(pl.multiple_of(rows.start + low, 16), 16)
                value = self.total[k, at].astype(WIDE)
                if self.near is not None:
                    value += self.near[1][k, at].astype(WIDE)
                for slot in slots:
                    value += self.land[slot, at].astype(WIDE)
                if place == (0, 0):
                    self.result[at] = value
                else:
                    self.stage[k, at] = value.astype(LOW)

            row_tiles(high - low, body)

    def settle(self, *place):
        if self.near is not None:
            self.near_copy(FAR_FIRST.index(place)).wait_recv()
        rest = BLOCK
        early = self.early.get(place)
        if early in self.ops:
            rest = self.cut
            self.blend(place, self.cut, BLOCK - self.cut, ())
            self.begin(early)
        names = [name for name in self.inward[place] if name in self.ops]
        for name in names:
            self.copy(name).wait_recv()
        self.blend(place, 0, rest, names)
        for name in self.outward[place]:
            if name in self.ops:
                self.begin(name)

    def drain(self):
        for name in self.started:
            self.copy(name).wait_send()
        if self.near is not None:
            for k in range(8):
                self.near_copy(k).wait_send()

    @staticmethod
    def scratch(columns, staged, near):
        part = pltpu.VMEM((8, BLOCK, columns), LOW)
        shapes = [pltpu.VMEM((8, BLOCK, columns), WIDE), part] if staged else [part]
        shapes += [part] + [pltpu.SemaphoreType.DMA((Reduce.COPIES,))] * 2
        return shapes + [part] * 2 if near else shapes


def normal_of(values):
    mean = jnp.mean(values, axis=-1, keepdims=True)
    centered = values - mean
    var = jnp.mean(centered * centered, axis=-1, keepdims=True)
    rstd = lax.rsqrt(var + EPSILON)
    return centered * rstd, rstd


def stack_heads(rows):
    lane = lax.broadcasted_iota(jnp.int32, rows.shape, 1)
    zero = jnp.zeros_like(rows)
    return jnp.concatenate(
        [jnp.where(lane < HDIM, rows, zero), jnp.where(lane < HDIM, zero, rows)], axis=0
    )


def causal_bias(chunk, block, tail_bias):
    key = block * KROWS + lax.broadcasted_iota(jnp.int32, (KROWS, 2 * QROWS), 0)
    lane = lax.broadcasted_iota(jnp.int32, (KROWS, 2 * QROWS), 1)
    query = chunk * QROWS + jnp.where(lane < QROWS, lane, lane - QROWS)
    own = jnp.where(block == 2048 // KROWS - 1, tail_bias, jnp.zeros_like(tail_bias))
    return jnp.where(key <= query, jnp.broadcast_to(own, key.shape), NEGATIVE)


def transpose_into(dst_ref, src_ref):
    rows = src_ref.shape[0]
    if rows <= 256:
        dst_ref[...] = src_ref[...].T
        return

    def body(i, carry):
        at = pl.multiple_of(i * 256, 256)
        dst_ref[:, pl.ds(at, 256)] = src_ref[pl.ds(at, 256), :].T
        return carry

    lax.fori_loop(0, rows // 256, body, 0)


def attend_chunk(chunk, q_ref, k_ref, vt_ref, mk_ref, mvt_ref, mem_bias, tail_bias):
    start = pl.multiple_of(chunk * QROWS, QROWS)
    q2 = stack_heads(q_ref[pl.ds(start, QROWS), :] * HDIM ** (-0.5))

    def values_times(values_t, probs):
        low = probs.astype(LOW)
        return (
            dot(values_t[:HDIM], low[:, :QROWS]),
            dot(values_t[HDIM:], low[:, QROWS:]),
        )

    scores = dot_nt(mk_ref[...], q2) + mem_bias
    peak = jnp.max(scores, axis=0, keepdims=True)
    raised = jnp.exp(scores - peak)
    total = jnp.sum(raised, axis=0, keepdims=True)
    first, second = values_times(mvt_ref[...], raised)

    def update(block, scores, carry):
        peak, total, first, second = carry
        at = pl.multiple_of(block * KROWS, KROWS)
        new_peak = jnp.maximum(peak, jnp.max(scores, axis=0, keepdims=True))
        scale = jnp.exp(peak - new_peak)
        raised = jnp.exp(scores - new_peak)
        total = total * scale + jnp.sum(raised, axis=0, keepdims=True)
        add_first, add_second = values_times(vt_ref[:, pl.ds(at, KROWS)], raised)
        return (
            new_peak,
            total,
            first * scale[:, :QROWS] + add_first,
            second * scale[:, QROWS:] + add_second,
        )

    def block_scores(block):
        at = pl.multiple_of(block * KROWS, KROWS)
        return dot_nt(k_ref[pl.ds(at, KROWS), :], q2)

    full = chunk * QROWS // KROWS
    carry = lax.fori_loop(
        0, full, lambda b, c: update(b, block_scores(b), c), (peak, total, first, second)
    )
    scores = block_scores(full) + causal_bias(chunk, full, tail_bias)
    peak, total, first, second = update(full, scores, carry)
    inverse = 1.0 / total
    attended = jnp.concatenate([first * inverse[:, :QROWS], second * inverse[:, QROWS:]], axis=0)
    return attended, peak + jnp.log(total)


def chip_at(group, order, step):
    return sum(jnp.where(step == j, group.chip(*place), 0) for j, place in enumerate(order))


def open_kernel(
    hidden_ref, cot_ref, memory_ref, gain_ref, shift_ref, w_ref, bias_ref,
    q_ref, k_ref, v_ref, mk_ref, mv_ref, mem_normed_ref, normed_out, cot_out,
    rows_buf, cot_buf, send, recv, cot_send, cot_recv, out_sem,
):
    head, seq = Group("head"), Group("seq")
    gather = Gather(head, rows_buf, send, recv)
    cot_gather = Gather(seq, cot_buf, cot_send, cot_recv)
    own, cot_own = head.block(0, 0), seq.block(0, 0)

    def norm_rows(rows):
        normal, _ = normal_of(hidden_ref[rows].astype(WIDE))
        rows_buf[own, rows] = (normal * gain_ref[...] + shift_ref[...]).astype(LOW)
        cot_buf[cot_own, rows] = cot_ref[rows]

    row_tiles(BLOCK, norm_rows, 32)
    greet_all(head, seq)
    gather.arrive(0, 0)
    cot_gather.arrive(0, 0)

    def norm_memory(rows):
        normal, _ = normal_of(memory_ref[rows].astype(WIDE))
        mem_normed_ref[rows] = (normal * gain_ref[...] + shift_ref[...]).astype(LOW)

    row_tiles(MEMROWS, norm_memory, 32)
    width = q_ref.shape[1]
    mem = (dot(mem_normed_ref[...], w_ref[:, width:]) + bias_ref[:, width:]).astype(LOW)
    mk_ref[...] = mem[:, :width]
    mv_ref[...] = mem[:, width:]
    copies = []

    def project(*place):
        gather.sibling(*place)
        chip = head.chip(*place)
        out = pltpu.make_async_copy(
            rows_buf.at[pl.ds(chip * 2, 2)], normed_out.at[pl.ds(chip * 2, 2)], out_sem.at[len(copies)]
        )
        out.start()
        copies.append(out)
        rows = rows_buf[pl.ds(chip * 2, 2)].reshape(2 * BLOCK, rows_buf.shape[2])
        at = pl.ds(pl.multiple_of(chip * 2 * BLOCK, 2 * BLOCK), 2 * BLOCK)
        for i, ref in enumerate((q_ref, k_ref, v_ref)):
            part = slice(i * width, (i + 1) * width)
            ref[at, :] = (dot(rows, w_ref[:, part]) + bias_ref[:, part]).astype(LOW)

    def keep_cot(*place):
        block = seq.block(*place)
        out = pltpu.make_async_copy(cot_buf.at[block], cot_out.at[block], out_sem.at[len(copies)])
        out.start()
        copies.append(out)

    project(0, 0)
    keep_cot(0, 0)
    gather.arrive(-1, 0)
    gather.arrive(1, 0)
    cot_gather.arrive(-1, 0)
    cot_gather.arrive(1, 0)
    gather.arrive(0, 1)
    cot_gather.arrive(0, 1)
    project(-1, 0)
    project(1, 0)
    gather.arrive(2, 0)
    cot_gather.arrive(2, 0)
    project(0, 1)
    gather.arrive(-1, 1)
    gather.arrive(1, 1)
    cot_gather.arrive(-1, 1)
    cot_gather.arrive(1, 1)
    project(2, 0)
    project(-1, 1)
    project(1, 1)
    gather.arrive(2, 1)
    cot_gather.arrive(2, 1)
    project(2, 1)
    for place in NEAR_FIRST[1:]:
        keep_cot(*place)
    gather.drain()
    cot_gather.drain()
    for out in copies:
        out.wait()


def open_layer(hidden, cot, memory, gain, shift, w, bias):
    rows, model = hidden.shape
    width = w.shape[1] // 3
    part = jax.ShapeDtypeStruct((16 * rows, width), LOW)
    mem_part = jax.ShapeDtypeStruct((MEMROWS, width), LOW)
    sems = [pltpu.SemaphoreType.DMA((Gather.COPIES,))] * 4
    return pl.pallas_call(
        open_kernel,
        out_shape=(
            part, part, part, mem_part, mem_part,
            jax.ShapeDtypeStruct((MEMROWS, model), LOW),
            jax.ShapeDtypeStruct((16, rows, model), LOW),
            jax.ShapeDtypeStruct((8, rows, model), LOW),
        ),
        in_specs=[VMEM] * 7,
        out_specs=(VMEM,) * 6 + (ANY,) * 2,
        scratch_shapes=[pltpu.VMEM((16, rows, model), LOW), pltpu.VMEM((8, rows, model), LOW)]
        + sems + [pltpu.SemaphoreType.DMA((16,))],
        compiler_params=pltpu.CompilerParams(
            collective_id=0, has_side_effects=True, vmem_limit_bytes=VMEM_LIMIT
        ),
        name="open_layer",
    )(hidden, cot, memory, gain, shift, w, bias)


def attend_kernel(
    q_ref, k_ref, v_ref, mk_ref, mv_ref, mem_bias_ref, tail_bias_ref, wo_ref,
    hidden_ref, b_out_ref, gain_ref, shift_ref,
    attn_t_ref, lse_ref, resid_ref, second_ref,
    vt_ref, mvt_ref, attn_ref, total, stage, land, send, recv, near_stage, near_land,
):
    head = Group("head")
    reduce = Reduce(head, total, stage, land, send, recv, 64, (near_stage, near_land), resid_ref)
    transpose_into(vt_ref, v_ref)
    transpose_into(mvt_ref, mv_ref)
    greet_all(head)

    def step(k, carry):
        chip = chip_at(head, FAR_FIRST, k)
        start = pl.multiple_of(chip * QROWS, QROWS)
        attended, lse = attend_chunk(
            chip, q_ref, k_ref, vt_ref, mk_ref, mvt_ref, mem_bias_ref[...], tail_bias_ref[...]
        )
        attn_t_ref[:, pl.ds(start, QROWS)] = attended.astype(LOW)
        attn_ref[...] = attended.T.astype(LOW)
        lse_ref[chip] = lse
        mine = attn_ref[pl.ds(pl.multiple_of(head.core * BLOCK, BLOCK), BLOCK), :]
        other = attn_ref[pl.ds(pl.multiple_of((1 - head.core) * BLOCK, BLOCK), BLOCK), :]
        for at in range(0, total.shape[2], 512):
            near_stage[k, :, at : at + 512] = dot(other, wo_ref[:, at : at + 512]).astype(LOW)
        reduce.near_copy(k).start()
        for at in range(0, total.shape[2], 512):
            total[k, :, at : at + 512] = dot(mine, wo_ref[:, at : at + 512])
        for j, place in enumerate(FAR_FIRST[:-1]):
            @pl.when(k == j + 1)
            def _():
                reduce.settle(*place)
        return carry

    lax.fori_loop(0, 8, step, 0)
    reduce.settle(0, 0)

    def finish(rows):
        resid = hidden_ref[rows].astype(WIDE) + resid_ref[rows] + b_out_ref[...]
        resid_ref[rows] = resid
        normal, _ = normal_of(resid)
        second_ref[rows] = (normal * gain_ref[...] + shift_ref[...]).astype(LOW)

    row_tiles(BLOCK, finish, 32)
    reduce.drain()


def attend_layer(q, k, v, mk, mv, mem_bias, tail_bias, wo, hidden, b_out, gain, shift):
    length, width = q.shape
    rows, model = hidden.shape
    return pl.pallas_call(
        attend_kernel,
        out_shape=(
            jax.ShapeDtypeStruct((width, length), LOW),
            jax.ShapeDtypeStruct((length // QROWS, 1, 2 * QROWS), WIDE),
            jax.ShapeDtypeStruct((rows, model), WIDE),
            jax.ShapeDtypeStruct((rows, model), LOW),
        ),
        in_specs=[VMEM] * 12,
        out_specs=(VMEM,) * 4,
        scratch_shapes=[
            pltpu.VMEM((width, length), LOW),
            pltpu.VMEM((width, MEMROWS), LOW),
            pltpu.VMEM((QROWS, width), LOW),
        ] + Reduce.scratch(model, True, True),
        compiler_params=pltpu.CompilerParams(
            collective_id=1, has_side_effects=True, vmem_limit_bytes=VMEM_LIMIT
        ),
        name="attend_layer",
    )(q, k, v, mk, mv, mem_bias, tail_bias, wo, hidden, b_out, gain, shift)


def gelu_parts(u):
    square = u * u
    t = jnp.tanh(0.7978845608 * (u + 0.044715 * (square * u)))
    half = 0.5 * (1.0 + t)
    slope = half + 0.5 * u * (1.0 - t * t) * (0.7978845608 * (1.0 + 0.134145 * square))
    return u * half, slope


def fold_rows(values):
    return jnp.sum(values.reshape(values.shape[0] // 8, 8, values.shape[1]), axis=0)


def feed_kernel(
    second_ref, w_up_hbm, w_down_hbm, up_bias_ref, cot_hbm, resid_ref, gain_ref, cot_ref,
    grad_resid_ref, sums_ref, branch_hbm, grad_w_ref, grad_b_up_ref,
    rows_buf, wu_ref, wd_ref, cot_buf, act_ref, back_ref, pre_ref, fold_ref, sum_fold, branch_buf,
    load_sem, branch_sem, send, recv,
    total, stage, land, rsend, rrecv,
    w_total, w_land, w_send, w_recv, w_near_stage, w_near_land,
):
    head, seq = Group("head"), Group("seq")
    gather = Gather(seq, rows_buf, send, recv, 64)
    reduce = Reduce(seq, total, stage, land, rsend, rrecv, 128, None, grad_resid_ref)
    w_reduce = Reduce(head, w_total, None, w_land, w_send, w_recv, 128, (w_near_stage, w_near_land), grad_w_ref)
    loads = [
        pltpu.make_async_copy(src, dst, load_sem.at[i])
        for i, (src, dst) in enumerate(
            ((cot_hbm, cot_buf), (w_down_hbm, wd_ref), (w_up_hbm, wu_ref))
        )
    ]
    for load in loads:
        load.start()
    own = seq.block(0, 0)
    rows_buf[own] = second_ref[...]
    fold_ref[...] = jnp.zeros_like(fold_ref)
    greet_all(head, seq)
    gather.arrive(0, 0)
    loads[0].wait()
    loads[1].wait()
    units = act_ref.shape[2]
    model = rows_buf.shape[2]

    def cot_times(i):
        pairs = cot_buf[pl.ds(2 * i, 2)].reshape(2 * BLOCK, model)
        for at in range(0, units, 256):
            part = dot_nt(pairs, wd_ref[at : at + 256, :]).astype(LOW)
            back_ref[pl.ds(2 * i, 2), :, at : at + 256] = part.reshape(2, BLOCK, 256)

    def feed(*place):
        block = seq.block(*place)
        pre_ref[...] = dot(rows_buf[block], wu_ref[...]) + up_bias_ref[...]

        def bend(rows):
            activated, slope = gelu_parts(pre_ref[rows])
            grad_pre = back_ref[block, rows].astype(WIDE) * slope
            act_ref[block, rows] = activated.astype(LOW)
            back_ref[block, rows] = grad_pre.astype(LOW)
            fold_ref[...] += fold_rows(grad_pre)

        row_tiles(BLOCK, bend)
        k = FAR_FIRST.index(place)
        for at in range(0, model, 512):
            total[k, :, at : at + 512] = dot_nt(back_ref[block], wu_ref[at : at + 512, :])

    cot_times(0)
    cot_times(1)
    loads[2].wait()
    cot_times(2)
    cot_times(3)
    feed(0, 0)
    gather.arrive(-1, 0)
    gather.arrive(1, 0)
    gather.arrive(0, 1)
    feed(-1, 0)
    gather.arrive(2, 0)
    feed(1, 0)
    gather.arrive(-1, 1)
    gather.arrive(1, 1)
    feed(0, 1)
    feed(2, 0)
    feed(-1, 1)
    feed(1, 1)
    gather.arrive(2, 1)
    feed(2, 1)
    reduce.settle(2, 1)
    reduce.settle(2, 0)
    grad_b_up_ref[...] = jnp.sum(fold_ref[...], axis=0, keepdims=True)

    def weights(k, carry):
        chip = chip_at(head, FAR_FIRST, k)

        def part(core):
            at = pl.ds(pl.multiple_of(chip * 2 * BLOCK + core * BLOCK, BLOCK), BLOCK)
            length = 8 * BLOCK
            up = dot_tn(
                rows_buf[:, :, at].reshape(length, BLOCK), back_ref[...].reshape(length, units)
            )
            down = dot_tn(
                cot_buf[:, :, at].reshape(length, BLOCK), act_ref[...].reshape(length, units)
            )
            return up.astype(LOW), down.astype(LOW)

        w_near_stage[k, :, :units], w_near_stage[k, :, units:] = part(1 - head.core)
        w_reduce.near_copy(k).start()
        w_total[k, :, :units], w_total[k, :, units:] = part(head.core)
        for j, place in enumerate(FAR_FIRST[:6]):
            @pl.when(k == j + 1)
            def _():
                w_reduce.settle(*place)

        @pl.when(k == 2)
        def _():
            reduce.settle(1, 1)
            reduce.settle(-1, 1)

        @pl.when(k == 5)
        def _():
            reduce.settle(1, 0)
            reduce.settle(-1, 0)

        return carry

    lax.fori_loop(0, 8, weights, 0)
    branch_copies = []

    def branch(i):
        slot = i % 2
        if i >= 2:
            branch_copies[i - 2].wait()
        for at in range(0, model, 512):
            branch_buf[slot, :, at : at + 512] = dot(act_ref[i], wd_ref[:, at : at + 512]).astype(LOW)
        copy = pltpu.make_async_copy(branch_buf.at[slot], branch_hbm.at[i], branch_sem.at[i])
        copy.start()
        branch_copies.append(copy)

    for i in range(4):
        branch(i)
    reduce.settle(0, 1)
    w_reduce.settle(0, 1)
    for i in range(4, 8):
        branch(i)
    reduce.settle(0, 0)
    sum_fold[...] = jnp.zeros_like(sum_fold)

    def back(rows):
        normal, rstd = normal_of(resid_ref[rows])
        incoming = grad_resid_ref[rows]
        scaled = incoming * gain_ref[...]
        inner = jnp.mean(scaled, axis=-1, keepdims=True)
        along = jnp.mean(scaled * normal, axis=-1, keepdims=True)
        cot = cot_ref[rows].astype(WIDE)
        grad = cot + rstd * (scaled - inner - normal * along)
        grad_resid_ref[rows] = grad
        for i, value in enumerate((grad, incoming * normal, incoming, cot)):
            sum_fold[i] += fold_rows(value)

    row_tiles(BLOCK, back)
    sums_ref[...] = jnp.sum(sum_fold[...], axis=1)
    w_reduce.settle(0, 0)
    for copy in branch_copies[-2:]:
        copy.wait()
    gather.drain()
    reduce.drain()
    w_reduce.drain()


def feed_layer(second, w_up, w_down, up_bias, cot_all, resid, gain, cot):
    rows, model = second.shape
    units = w_up.shape[1]
    gather_sems = [pltpu.SemaphoreType.DMA((Gather.COPIES,))] * 2
    return pl.pallas_call(
        feed_kernel,
        out_shape=(
            jax.ShapeDtypeStruct((rows, model), WIDE),
            jax.ShapeDtypeStruct((4, model), WIDE),
            jax.ShapeDtypeStruct((8, rows, model), LOW),
            jax.ShapeDtypeStruct((rows, 2 * units), WIDE),
            jax.ShapeDtypeStruct((1, units), WIDE),
        ),
        in_specs=[VMEM, ANY, ANY, VMEM, ANY, VMEM, VMEM, VMEM],
        out_specs=(VMEM, VMEM, ANY, VMEM, VMEM),
        scratch_shapes=[
            pltpu.VMEM((8, rows, model), LOW),
            pltpu.VMEM((model, units), LOW),
            pltpu.VMEM((units, model), LOW),
            pltpu.VMEM((8, rows, model), LOW),
            pltpu.VMEM((8, rows, units), LOW),
            pltpu.VMEM((8, rows, units), LOW),
            pltpu.VMEM((rows, units), WIDE),
            pltpu.VMEM((8, units), WIDE),
            pltpu.VMEM((4, 8, model), WIDE),
            pltpu.VMEM((2, rows, model), LOW),
            pltpu.SemaphoreType.DMA((3,)),
            pltpu.SemaphoreType.DMA((8,)),
        ] + gather_sems + Reduce.scratch(model, True, False) + Reduce.scratch(2 * units, False, True),
        compiler_params=pltpu.CompilerParams(
            collective_id=2, has_side_effects=True, vmem_limit_bytes=VMEM_LIMIT
        ),
        name="feed_layer",
    )(second, w_up, w_down, up_bias, cot_all, resid, gain, cot)


def attend_back_chunk(
    chunk, q_ref, k_ref, kt_ref, v_ref, mk_ref, mkt_ref, mv_ref, mem_bias, tail_bias,
    attn_t_ref, lse_ref, grad_rows, dk_ref, dv_ref, dmk_ref, dmv_ref,
):
    start = pl.multiple_of(chunk * QROWS, QROWS)
    q2 = stack_heads(q_ref[pl.ds(start, QROWS), :] * HDIM ** (-0.5))
    g2 = stack_heads(grad_rows)
    product = grad_rows.astype(WIDE).T * attn_t_ref[:, pl.ds(start, QROWS)].astype(WIDE)
    inner = jnp.concatenate(
        [
            jnp.sum(product[:HDIM], axis=0, keepdims=True),
            jnp.sum(product[HDIM:], axis=0, keepdims=True),
        ],
        axis=1,
    )
    lse = lse_ref[chunk]

    def piece(scores, values, keys_t):
        probs = jnp.exp(scores - lse)
        grad_probs = dot_nt(values, g2)
        grad_scores = (probs * (grad_probs - inner)).astype(LOW)
        return (
            dot(probs.astype(LOW), g2),
            dot(grad_scores, q2),
            dot(keys_t[:HDIM], grad_scores[:, :QROWS]),
            dot(keys_t[HDIM:], grad_scores[:, QROWS:]),
        )

    dv, dk, first, second = piece(
        dot_nt(mk_ref[...], q2) + mem_bias, mv_ref[...], mkt_ref[...]
    )
    dmv_ref[...] += dv
    dmk_ref[...] += dk

    def block_step(block, bias, carry):
        first, second = carry
        at = pl.multiple_of(block * KROWS, KROWS)
        scores = dot_nt(k_ref[pl.ds(at, KROWS), :], q2)
        if bias is not None:
            scores = scores + bias
        dv, dk, add_first, add_second = piece(
            scores, v_ref[pl.ds(at, KROWS), :], kt_ref[:, pl.ds(at, KROWS)]
        )
        dv_ref[pl.ds(at, KROWS), :] += dv
        dk_ref[pl.ds(at, KROWS), :] += dk
        return first + add_first, second + add_second

    full = chunk * QROWS // KROWS
    carry = lax.fori_loop(0, full, lambda b, c: block_step(b, None, c), (first, second))
    first, second = block_step(full, causal_bias(chunk, full, tail_bias), carry)
    return jnp.concatenate([first, second], axis=0) * HDIM ** (-0.5)


def grad_kernel(
    grad_resid_ref, resid_ref, b_down_ref, branch_hbm, wo_ref,
    q_ref, k_ref, v_ref, mk_ref, mv_ref, mem_bias_ref, tail_bias_ref, attn_t_ref, lse_ref,
    out_ref, own_ref, own_t_ref, mem_ref, mem_t_ref, grad_wo_ref, sums_ref,
    rows_buf, kt_ref, mkt_ref, dk_ref, dv_ref, dmk_ref, dmv_ref, wo_sum, branch_sum, fold_ref,
    load_sem, send, recv, total, land, rsend, rrecv,
):
    head, seq = Group("head"), Group("seq")
    gather = Gather(head, rows_buf, send, recv, 112)
    reduce = Reduce(seq, total, None, land, rsend, rrecv, 128, None, branch_sum)
    loads = [
        pltpu.make_async_copy(branch_hbm.at[seq.block(*place)], total.at[k], load_sem.at[k])
        for k, place in enumerate(FAR_FIRST)
    ]
    for load in loads:
        load.start()
    own = head.block(0, 0)
    rows_buf[own] = grad_resid_ref[...].astype(LOW)
    greet_all(head, seq)
    gather.arrive(0, 0)
    loads[0].wait()
    reduce.settle(2, 1)
    loads[1].wait()
    reduce.settle(2, 0)
    transpose_into(kt_ref, k_ref)
    transpose_into(mkt_ref, mk_ref)
    for ref in (dk_ref, dv_ref, dmk_ref, dmv_ref, wo_sum, fold_ref):
        ref[...] = jnp.zeros_like(ref)
    width, model = wo_ref.shape
    for load in loads[2:]:
        load.wait()

    def step(k, carry):
        @pl.when(k == 0)
        def _():
            gather.sibling(0, 0)

        @pl.when(k == 1)
        def _():
            gather.arrive(-1, 0)
            gather.arrive(1, 0)
            reduce.settle(1, 1)
            reduce.settle(-1, 1)
            gather.arrive(0, 1)
            gather.sibling(-1, 0)

        @pl.when(k == 2)
        def _():
            reduce.settle(1, 0)
            reduce.settle(-1, 0)
            gather.sibling(1, 0)

        @pl.when(k == 3)
        def _():
            gather.arrive(2, 0)
            gather.sibling(0, 1)

        @pl.when(k == 4)
        def _():
            gather.arrive(-1, 1)
            gather.arrive(1, 1)
            gather.sibling(2, 0)

        @pl.when(k == 5)
        def _():
            reduce.settle(0, 1)
            gather.sibling(-1, 1)

        @pl.when(k == 6)
        def _():
            gather.arrive(2, 1)
            gather.sibling(1, 1)

        @pl.when(k == 7)
        def _():
            gather.sibling(2, 1)

        chip = chip_at(head, NEAR_FIRST, k)
        at = pl.ds(pl.multiple_of(chip * QROWS, QROWS), QROWS)
        rows = rows_buf[pl.ds(chip * 2, 2)].reshape(QROWS, model)
        grad_rows = dot_nt(rows, wo_ref[...]).astype(LOW)
        wo_sum[...] += dot(attn_t_ref[:, at], rows)
        dq = attend_back_chunk(
            chip, q_ref, k_ref, kt_ref, v_ref, mk_ref, mkt_ref, mv_ref,
            mem_bias_ref[...], tail_bias_ref[...], attn_t_ref, lse_ref,
            grad_rows, dk_ref, dv_ref, dmk_ref, dmv_ref,
        ).astype(LOW)
        own_t_ref[:width, at] = dq
        own_ref[at, :width] = dq.T
        return carry

    lax.fori_loop(0, 8, step, 0)

    def finish_keys(i, carry):
        at = pl.ds(pl.multiple_of(i * 256, 256), 256)
        dk = dk_ref[at, :].astype(LOW)
        dv = dv_ref[at, :].astype(LOW)
        own_ref[at, width : 2 * width] = dk
        own_ref[at, 2 * width :] = dv
        own_t_ref[width : 2 * width, at] = dk.T
        own_t_ref[2 * width :, at] = dv.T
        fold_ref[...] += fold_rows(own_ref[at, :].astype(WIDE))
        return carry

    lax.fori_loop(0, q_ref.shape[0] // 256, finish_keys, 0)
    for i, ref in enumerate((dmk_ref, dmv_ref)):
        low = ref[...].astype(LOW)
        mem_ref[:, i * width : (i + 1) * width] = low
        mem_t_ref[i * width : (i + 1) * width, :] = low.T
    fold_ref[:, width:] += fold_rows(mem_ref[...].astype(WIDE))
    sums_ref[...] = jnp.sum(fold_ref[...], axis=0, keepdims=True)
    grad_wo_ref[...] = wo_sum[...].astype(LOW)
    reduce.settle(0, 0)

    def finish(rows):
        out_ref[rows] = (resid_ref[rows] + branch_sum[rows] + b_down_ref[...]).astype(LOW)

    row_tiles(BLOCK, finish)
    gather.drain()
    reduce.drain()


def grad_layer(
    grad_resid, resid, b_down, branch, wo, q, k, v, mk, mv, mem_bias, tail_bias, attn_t, lse
):
    rows, model = grad_resid.shape
    length, width = q.shape
    return pl.pallas_call(
        grad_kernel,
        out_shape=(
            jax.ShapeDtypeStruct((rows, model), LOW),
            jax.ShapeDtypeStruct((length, 3 * width), LOW),
            jax.ShapeDtypeStruct((3 * width, length), LOW),
            jax.ShapeDtypeStruct((MEMROWS, 2 * width), LOW),
            jax.ShapeDtypeStruct((2 * width, MEMROWS), LOW),
            jax.ShapeDtypeStruct((width, model), LOW),
            jax.ShapeDtypeStruct((1, 3 * width), WIDE),
        ),
        in_specs=[VMEM] * 3 + [ANY] + [VMEM] * 10,
        out_specs=(VMEM,) * 7,
        scratch_shapes=[
            pltpu.VMEM((16, rows, model), LOW),
            pltpu.VMEM((width, length), LOW),
            pltpu.VMEM((width, MEMROWS), LOW),
            pltpu.VMEM((length, width), WIDE),
            pltpu.VMEM((length, width), WIDE),
            pltpu.VMEM((MEMROWS, width), WIDE),
            pltpu.VMEM((MEMROWS, width), WIDE),
            pltpu.VMEM((width, model), WIDE),
            pltpu.VMEM((rows, model), WIDE),
            pltpu.VMEM((8, 3 * width), WIDE),
            pltpu.SemaphoreType.DMA((8,)),
        ] + [pltpu.SemaphoreType.DMA((Gather.COPIES,))] * 2 + Reduce.scratch(model, False, False),
        compiler_params=pltpu.CompilerParams(
            collective_id=3, has_side_effects=True, vmem_limit_bytes=VMEM_LIMIT
        ),
        name="grad_layer",
    )(grad_resid, resid, b_down, branch, wo, q, k, v, mk, mv, mem_bias, tail_bias, attn_t, lse)


def close_kernel(
    own_ref, own_t_ref, mem_t_ref, grad_wo_ref, mem_normed_ref, normed_hbm, w_ref,
    hidden_ref, gain_ref, grad_resid_ref,
    grad_hidden_ref, grad_w_ref, sums_ref,
    rows_buf, mem_pad, sum_fold, load_sem,
    total, stage, land, send, recv, near_stage, near_land,
    w_total, w_stage, w_land, w_send, w_recv, w_buf, g_send, g_recv,
):
    head, seq = Group("head"), Group("seq")
    reduce = Reduce(head, total, stage, land, send, recv, 112, (near_stage, near_land), grad_hidden_ref)
    w_reduce = Reduce(seq, w_total, w_stage, w_land, w_send, w_recv, 128, None, w_total.at[7])
    gather = Gather(seq, w_buf, g_send, g_recv, 96)
    load = pltpu.make_async_copy(normed_hbm, rows_buf, load_sem)
    load.start()
    width = grad_wo_ref.shape[0]
    model = rows_buf.shape[2]
    length = own_ref.shape[0]
    wide = model // 2
    mem_pad[...] = jnp.zeros_like(mem_pad)
    mem_pad[pl.ds(width, 2 * width), :] = mem_t_ref[...]
    greet_all(head, seq)

    def chunk(k):
        chip = chip_at(head, FAR_FIRST, k)

        def part(core):
            at = pl.ds(pl.multiple_of(chip * QROWS + core * BLOCK, BLOCK), BLOCK)
            return own_ref[at, :]

        mine, other = part(head.core), part(1 - head.core)
        for at in range(0, model, 512):
            near_stage[k, :, at : at + 512] = dot_nt(other, w_ref[at : at + 512, :]).astype(LOW)
        reduce.near_copy(k).start()
        for at in range(0, model, 512):
            total[k, :, at : at + 512] = dot_nt(mine, w_ref[at : at + 512, :])

    def weights(k):
        target = chip_at(seq, FAR_FIRST, k)
        part, side = target // 2, target % 2
        columns = pl.ds(pl.multiple_of(side * wide, wide), wide)

        @pl.when(part < 3)
        def _():
            at = pl.ds(pl.multiple_of(part * width, width), width)
            w_total[k] = dot(
                own_t_ref[at, :], rows_buf[:, :, columns].reshape(length, wide)
            ) + dot(mem_pad[at, :], mem_normed_ref[:, columns])

        @pl.when(part == 3)
        def _():
            w_total[k] = grad_wo_ref[:, columns].astype(WIDE)

    def step(k, carry):
        chunk(k)

        @pl.when(k == 0)
        def _():
            load.wait()

        weights(k)
        for j, place in enumerate(FAR_FIRST[:6]):
            @pl.when(k == j + 1)
            def _():
                reduce.settle(*place)
                if j < 4:
                    w_reduce.settle(*place)
        return carry

    lax.fori_loop(0, 8, step, 0)
    w_reduce.settle(1, 0)
    w_reduce.settle(-1, 0)
    w_reduce.settle(0, 1)
    reduce.settle(0, 1)
    w_reduce.settle(0, 0)
    own = seq.block(0, 0)
    w_buf[own] = w_total[7].astype(LOW)
    gather.arrive(0, 0)
    gather.arrive(-1, 0)
    gather.arrive(1, 0)
    gather.arrive(0, 1)
    reduce.settle(0, 0)
    sum_fold[...] = jnp.zeros_like(sum_fold)

    def back(rows):
        normal, rstd = normal_of(hidden_ref[rows].astype(WIDE))
        incoming = grad_hidden_ref[rows]
        scaled = incoming * gain_ref[...]
        inner = jnp.mean(scaled, axis=-1, keepdims=True)
        along = jnp.mean(scaled * normal, axis=-1, keepdims=True)
        grad_hidden_ref[rows] = grad_resid_ref[rows] + rstd * (scaled - inner - normal * along)
        for i, value in enumerate((incoming * normal, incoming)):
            sum_fold[i] += fold_rows(value)

    row_tiles(BLOCK, back)
    sums_ref[...] = jnp.sum(sum_fold[...], axis=1)
    for place in NEAR_FIRST[4:]:
        gather.arrive(*place)
    grad_w_ref[...] = w_buf[...]
    gather.drain()
    w_reduce.drain()
    reduce.drain()


def close_layer(own, own_t, mem_t, grad_wo, mem_normed, normed_all, w, hidden, gain, grad_resid):
    rows, model = hidden.shape
    width = grad_wo.shape[0]
    sems = [pltpu.SemaphoreType.DMA((Gather.COPIES,))] * 2
    return pl.pallas_call(
        close_kernel,
        out_shape=(
            jax.ShapeDtypeStruct((rows, model), WIDE),
            jax.ShapeDtypeStruct((8, width, model // 2), LOW),
            jax.ShapeDtypeStruct((2, model), WIDE),
        ),
        in_specs=[VMEM] * 5 + [ANY] + [VMEM] * 4,
        out_specs=(VMEM,) * 3,
        scratch_shapes=[
            pltpu.VMEM((16, rows, model), LOW),
            pltpu.VMEM((3 * width, MEMROWS), LOW),
            pltpu.VMEM((2, 8, model), WIDE),
            pltpu.SemaphoreType.DMA,
        ] + Reduce.scratch(model, True, True) + Reduce.scratch(model // 2, True, False)
        + [pltpu.VMEM((8, width, model // 2), LOW)] + sems,
        compiler_params=pltpu.CompilerParams(
            collective_id=4, has_side_effects=True, vmem_limit_bytes=VMEM_LIMIT
        ),
        name="close_layer",
    )(own, own_t, mem_t, grad_wo, mem_normed, normed_all, w, hidden, gain, grad_resid)


def norm_back(values, gain, incoming):
    normal, rstd = normal_of(values)
    scaled = incoming * gain
    inner = jnp.mean(scaled, axis=-1, keepdims=True)
    along = jnp.mean(scaled * normal, axis=-1, keepdims=True)
    return (
        rstd * (scaled - inner - normal * along),
        jnp.sum(incoming * normal, axis=0),
        jnp.sum(incoming, axis=0),
    )


def on_device(
    hidden, memory, counts, w_qkv, b_query, b_value, output_weight, b_out,
    gain_one, shift_one, gain_two, shift_two, w_up, up_bias, w_down, b_down, cotangent,
):
    hidden, memory, cot = hidden[:, 0], memory[:, 0], cotangent[:, 0]
    slots, model = memory.shape
    width, units = w_qkv.shape[2], w_up.shape[1]
    seq_index = lax.axis_index("seq")
    memory = jnp.pad(memory, ((0, MEMROWS - slots), (0, 0)))
    flat_w = w_qkv.reshape(model, 3 * width)
    flat_bias = jnp.concatenate([b_query, jnp.zeros_like(b_query), b_value])[None]
    gain_one, shift_one, gain_two, shift_two, b_out, b_down = (
        vector[None] for vector in (gain_one, shift_one, gain_two, shift_two, b_out, b_down)
    )
    slot = jnp.arange(MEMROWS, dtype=jnp.int32)
    mem_bias = jnp.where(slot < counts[0, 0], 0.0, NEGATIVE).astype(WIDE)[:, None]
    length = 16 * hidden.shape[0]
    position = length - KROWS + jnp.arange(KROWS, dtype=jnp.int32)
    text_rows = length - slots
    own_ok = (position < text_rows) | (position - text_rows < counts[0, 1])
    tail_bias = jnp.where(own_ok, 0.0, NEGATIVE).astype(WIDE)[:, None]
    up_bias_own = lax.dynamic_slice(up_bias, (seq_index * units,), (units,))[None]

    q, k, v, mk, mv, mem_normed, normed_all, cot_all = open_layer(
        hidden, cot, memory, gain_one, shift_one, flat_w, flat_bias
    )
    attn_t, lse, resid, second = attend_layer(
        q, k, v, mk, mv, mem_bias, tail_bias, output_weight, hidden, b_out, gain_two, shift_two
    )
    grad_resid, feed_sums, branch, grad_w, grad_b_up = feed_layer(
        second, w_up, w_down, up_bias_own, cot_all, resid, gain_two, cot
    )
    output, own, own_t, mem, mem_t, grad_wo, bias_sums = grad_layer(
        grad_resid, resid, b_down, branch, output_weight,
        q, k, v, mk, mv, mem_bias, tail_bias, attn_t, lse,
    )
    grad_mem_normed = dot_nt(mem, flat_w[:, width:])
    memory_back, gain_states, shift_states = norm_back(
        memory.astype(WIDE), gain_one, grad_mem_normed
    )
    grad_memory = lax.psum(memory_back[:slots].astype(LOW), "head").astype(WIDE)
    bias_sums = lax.psum(bias_sums[0].astype(LOW), "seq").astype(WIDE)
    grad_hidden, grad_heads, norm_sums = close_layer(
        own, own_t, mem_t, grad_wo, mem_normed, normed_all, flat_w, hidden, gain_one, grad_resid
    )
    grad_heads = grad_heads.reshape(4, 2, width, model // 2).transpose(1, 3, 0, 2)
    grad_heads = grad_heads.reshape(model, 4, width).astype(WIDE)
    grad_b_up = lax.dynamic_update_slice(
        jnp.zeros(up_bias.shape, WIDE), grad_b_up[0], (seq_index * units,)
    )
    totals = lax.psum(
        jnp.concatenate(
            [
                feed_sums[0],
                norm_sums[0] + gain_states,
                norm_sums[1] + shift_states,
                feed_sums[1],
                feed_sums[2],
                feed_sums[3],
                grad_b_up,
            ]
        ),
        ("head", "seq"),
    )
    sums = [totals[i * model : (i + 1) * model] for i in range(6)]
    return (
        output[:, None],
        grad_hidden[:, None],
        grad_memory[:, None],
        grad_heads[:, :3],
        bias_sums[:width],
        bias_sums[2 * width :],
        grad_heads[:, 3].T,
        sums[0],
        sums[1],
        sums[2],
        sums[3],
        sums[4],
        grad_w[:, :units],
        totals[6 * model :],
        grad_w[:, units:].T,
        sums[5],
    )


def solution(mesh):
    return jax.shard_map(
        on_device,
        mesh=mesh,
        in_specs=(
            P("head", "seq", None),
            P(None, "seq", None),
            P("seq", None),
            P(None, None, "head"),
            P("head"),
            P("head"),
            P("head", None),
            P(),
            P(),
            P(),
            P(),
            P(),
            P(None, "seq"),
            P(),
            P("seq", None),
            P(),
            P("head", "seq", None),
        ),
        out_specs=(
            P("head", "seq", None),
            P("head", "seq", None),
            P(None, "seq", None),
            P(None, None, "head"),
            P("head"),
            P("head"),
            P("head", None),
            P(),
            P(),
            P(),
            P(),
            P(),
            P("head", "seq"),
            P(),
            P("seq", "head"),
            P(),
        ),
        check_vma=False,
    )
```

time: 2650 us -> 631 us (0.24)
  waiting for transfers between devices: 2120 us -> 244 us
  Pallas kernels: 0 us -> 315 us
  matrix products: 263 us -> 0.47 us
  other arithmetic: 105 us -> 6.91 us
  local copies, waits for them, and re-layouts: 91.3 us -> 26.1 us
    all_gather x4 -> x0, waiting for transfers between devices: 1000 us -> none  [the longest x1 625 us: on_device(): lax.all_gather(w_down, 'seq', axis=0, tiled=True)]
    reduce_scatter x5 -> x0, waiting for transfers between devices: 808 us -> none  [the longest x1 361 us: on_device(): lax.psum_scatter(jnp.einsum('wpy,yo->wpo', partial_rows, output_weight, p...]
    pallas_call x0 -> x5, Pallas kernels: none -> 315 us  [the longest x1 96.1 us: feed_layer(): pl.pallas_call(feed_kernel, out_shape=(jax.ShapeDtypeStruct((rows, model)...]
    dot_general x42 -> x1, matrix products: 262 us -> 0.47 us  [dot_nt(): lax.dot_general(left, right, (((1,), (1,)), ((), ())), preferred_element_...]
    convert_element_type x12 -> x1, other arithmetic: 49.1 us -> 0.02 us  [on_device(): bias_sums = lax.psum(bias_sums[0].astype(LOW), 'seq').astype(WIDE)]
    unnamed x103 -> x32, local copies, waits for them, and re-layouts: 59.7 us -> 11.9 us
    unnamed x14 -> x2, waiting for transfers between devices: 33.7 us -> 0.03 us
    psum x3 -> x2, waiting for transfers between devices: 277 us -> 244 us  [the longest x1 131 us: on_device(): grad_memory = lax.psum(memory_back[:slots].astype(LOW), 'head').astype(WIDE)]
  transfers between devices with their start and end apart: 13 -> 2, of which waited for: 13 -> 2; matrix products, arithmetic and copies ran while one was open for 13% -> 3% of each run, Pallas kernels for 0% -> 0%
where the time goes in v1:
time: 631 us; the launch traced here: 621 us
  Pallas kernels  315 us (50%)
  waiting for transfers between devices  244 us (39%)
  local copies, waits for them, and re-layouts  26.1 us (4%)
  between operations  14.7 us (2%)
  blocking collectives  13.9 us (2%)
  other arithmetic  6.91 us (1%)
    psum x1, waiting for transfers between devices, on_device(): grad_memory = lax.psum(memory_back[:slots].astype(LOW), 'head').astype(WIDE)  131 us
    psum x1, waiting for transfers between devices, on_device(): lax.psum(jnp.concatenate([feed_sums[0], norm_sums[0] + gain_states, norm_...  113 us
    pallas_call x1, Pallas kernels, feed_layer(): pl.pallas_call(feed_kernel, out_shape=(jax.ShapeDtypeStruct((rows, model)...  96.1 us
    pallas_call x1, Pallas kernels, close_layer(): pl.pallas_call(close_kernel, out_shape=(jax.ShapeDtypeStruct((rows, model...  58.2 us
    pallas_call x1, Pallas kernels, open_layer(): pl.pallas_call(open_kernel, out_shape=(part, part, part, mem_part, mem_pa...  55.5 us
    pallas_call x1, Pallas kernels, grad_layer(): pl.pallas_call(grad_kernel, out_shape=(jax.ShapeDtypeStruct((rows, model)...  55 us
    pallas_call x1, Pallas kernels, attend_layer(): pl.pallas_call(attend_kernel, out_shape=(jax.ShapeDtypeStruct((width, len...  50 us
    psum x1, blocking collectives, on_device(): bias_sums = lax.psum(bias_sums[0].astype(LOW), 'seq').astype(WIDE)  13.9 us
  transfers between devices with their start and end apart: 2, of which 2 were waited for; matrix products, arithmetic and copies ran while one was open for 3% of the time, Pallas kernels for 0%

profile of v1, /device:TPU:1, one launch (start us, length us, event | category | flops | bytes accessed | tf_op | source)
XLA Modules:
  0.0 621.2 jit_solution(15712844959820671562)
XLA Ops:
  7.2 0.0 all-reduce.6.cloned.1.call-start
  7.2 1.1 convert_reduce_fusion
  8.3 1.7 pad.4.memory_ref
  10.0 1.8 copy.39
  11.7 1.6 copy.40.w_ref
  13.3 0.0 copy-done.8
  13.3 0.0 copy-done.9
  13.3 0.6 broadcast_in_dim.67.bias_ref
  13.9 0.0 copy-done.6
  13.9 0.6 fusion.18
  14.5 1.4 fusion.9.tail_bias_ref
  15.9 1.3 fusion.11.mem_bias_ref
  17.2 1.3 dynamic_slice.3
  18.4 55.5 %open_layer.1 = (bf16[2048,128]{1,0:T(8,128)(2,1)}, bf16[2048,128]{1,0:T(8,128)(2,1)}, bf16[2048,128]{1,0:T(8,128)(2,1)}, bf16[64,128]{1,0:T(8,128)(2,1)}, bf16[...) custom-call(bf16[128,2048]{1,0:T(8,128)(2,1)} %bitcast.44, ...), custom_call_target="tpu_custom_call" | custom-call | tf_op jit(solution)/shard_map/open_layer/pallas_call | solution.py:471
  73.9 50.0 %attend_layer.1 = (bf16[128,2048]{1,0:T(8,128)(2,1)}, f32[8,1,512]{2,1,0:T(1,128)}, f32[128,2048]{1,0:T(8,128)}, bf16[128,2048]{1,0:T(8,128)(2,1)}) custom-call(bf16[2048,128]{1,0:T(8,128)(2,1)} %get-tuple-element.43.q_ref, bf16[2048,128]{1,0:T(8,128)(2,1)} %get-tuple-element.44.k_ref, bf16[2048,128]{1,0:T(8,128)(2,1)} %get-tuple-element.45.v_ref, ...), custom_call_target="tpu_custom_call" | custom-call | tf_op jit(solution)/shard_map/attend_layer/pallas_call | solution.py:540
  123.9 96.1 %feed_layer.1 = (f32[128,2048]{1,0:T(8,128)}, f32[4,2048]{1,0:T(4,128)}, bf16[8,128,2048]{2,1,0:T(8,128)(2,1)}, f32[128,2048]{1,0:T(8,128)}, f32[1,1024]{1,0:T(1,128)}) custom-call(bf16[128,2048]{1,0:T(8,128)(2,1)} %get-tuple-element.48.second_ref, bf16[2048,1024]{1,0:T(8,128)(2,1)} %w_up_hbm.1, bf16[1024,2048]{1,0:T(8,128)(2,1)} %w_down_hbm.1, ...), custom_call_target="tpu_custom_call" | custom-call | tf_op jit(solution)/shard_map/feed_layer/pallas_call | solution.py:732
  220.0 55.0 %grad_layer.1 = (bf16[128,2048]{1,0:T(8,128)(2,1)}, bf16[2048,384]{1,0:T(8,128)(2,1)}, bf16[384,2048]{1,0:T(8,128)(2,1)}, bf16[64,256]{1,0:T(8,128)(2,1)}, bf16[...) custom-call(f32[128,2048]{1,0:T(8,128)} %get-tuple-element.51.grad_resid_ref, ...), custom_call_target="tpu_custom_call" | custom-call | tf_op jit(solution)/shard_map/grad_layer/pallas_call | solution.py:944
  275.0 0.0 copy-start
  275.0 0.0 copy-start.3
  275.1 0.0 copy-start.10
  275.1 0.0 copy-start.5
  275.1 58.2 %close_layer.1 = (f32[128,2048]{1,0:T(8,128)}, bf16[8,128,1024]{2,1,0:T(8,128)(2,1)}, f32[2,2048]{1,0:T(2,128)}) custom-call(bf16[2048,384]{1,0:T(8,128)(2,1)} %get-tuple-element.56.own_ref, bf16[384,2048]{1,0:T(8,128)(2,1)} %get-tuple-element.57.own_t_ref, bf16[256,64]{1,0:T(8,128)(2,1)} %get-tuple-element.58.mem_t_ref, ...), custom_call_target="tpu_custom_call" | custom-call | tf_op jit(solution)/shard_map/close_layer/pallas_call | solution.py:1084
  333.3 0.8 fusion.16
  334.2 0.2 fusion.4
  334.5 0.5 fusion.12
  335.0 0.3 dynamic_update_slice.3
  335.3 0.6 copy-done.2
  336.0 0.0 all-reduce.6.cloned.1.call-update
  336.0 0.0 all-reduce.4.cloned.1.call-start
  336.1 0.8 fusion.10
  336.9 0.0 all-reduce.4.cloned.1.call-update
  336.9 2.0 convert_bitcast_fusion
  339.0 0.6 copy.47
  339.6 0.3 slice.99
  339.9 1.0 slice_bitcast_fusion
  341.0 2.4 copy.45
  343.3 3.3 copy.43
  346.7 13.9 %psum.22 = bf16[384]{0:T(512)(128)(2,1)S(1)} all-reduce(bf16[384]{0:T(512)(128)(2,1)S(1)} %convert_reduce_fusion.1), channel_id=1, replica_groups=mesh['head'=16,'seq'=8] {'seq'}, use_global_device_ids=true, to_apply=%region_5.6 | all-reduce | flops 384 | bytes 1536 | tf_op jit(solution)/shard_map/psum | solution.py:1160
  360.6 0.5 fusion.17
  361.1 2.1 slice_bitcast_fusion.1
  363.2 1.0 copy.46
  364.2 112.9 %all-reduce.6.cloned.1.call-done = f32[20480]{0:T(1024)} async-done(((f32[20480]{0:T(1024)}), f32[20480]{0:T(1024)}) %all-reduce.6.cloned.1.call-update) | async-done | bytes 81936 | tf_op jit(solution)/shard_map/psum | solution.py:1169
  477.1 1.4 slice.106
  478.4 1.4 fusion.14
  479.9 131.2 %all-reduce.4.cloned.1.call-done = bf16[50,1,2048]{2,0,1:T(8,128)(2,1)} async-done(((bf16[50,1,2048]{2,0,1:T(8,128)(2,1)}), bf16[50,1,2048]{2,0,1:T(8,128)(2,1)}) %all-reduce.4.cloned.1.call-update) | async-done | bytes 204816 | tf_op jit(solution)/shard_map/psum | solution.py:1159
  611.1 2.0 copy.44
  613.1 0.0 copy-done.1
  613.1 0.8 copy.58
  (28 shorter events, 0.1 us)
Async XLA Ops:
  7.2 469.9 %all-reduce.6.cloned.1.call-start = ((), (), s32[]{:S(2)}) async-start(), calls=%async_computation.1 | async-start | bytes 163840 | tf_op jit(solution)/shard_map/psum | solution.py:1169
  10.0 3.3 copy-start.8
  10.0 3.3 copy-start.9
  10.0 3.9 copy-start.6
  275.0 59.1 %copy-start = (bf16[50,1,2048]{2,0,1:T(8,128)(2,1)S(1)}, bf16[50,1,2048]{2,0,1:T(8,128)(2,1)}, u32[]{:S(2)}) copy-start(bf16[50,1,2048]{2,0,1:T(8,128)(2,1)} %param.18) | copy-start | bytes 614404
  275.0 59.4 %copy-start.4 = (f32[4,2048]{1,0:T(4,128)S(1)}, f32[4,2048]{1,0:T(4,128)}, u32[]{:S(2)}) copy-start(f32[4,2048]{1,0:T(4,128)} %get-tuple-element.66) | copy-start | bytes 98308
  275.0 59.4 %copy-start.3 = (f32[2048]{0:T(1024)S(1)}, f32[2048]{0:T(1024)}, u32[]{:S(2)}) copy-start(f32[2048]{0:T(1024)} %param.25) | copy-start | bytes 24580
  275.1 59.4 %copy-start.10 = (bf16[64,256]{1,0:T(8,128)(2,1)S(1)}, bf16[64,256]{1,0:T(8,128)(2,1)}, u32[]{:S(2)}) copy-start(bf16[64,256]{1,0:T(8,128)(2,1)} %get-tuple-element.63) | copy-start | bytes 98308
  275.1 60.0 %copy-start.5 = (f32[1,1024]{1,0:T(1,128)S(1)}, f32[1,1024]{1,0:T(1,128)}, u32[]{:S(2)}) copy-start(f32[1,1024]{1,0:T(1,128)} %get-tuple-element.68) | copy-start | bytes 12292
  335.3 0.6 copy-start.2
  336.0 275.1 %all-reduce.4.cloned.1.call-start = ((), (), s32[]{:S(2)}) async-start(), calls=%async_computation | async-start | bytes 458752 | tf_op jit(solution)/shard_map/psum | solution.py:1159
  341.0 5.7 copy-start.7
  343.3 269.8 %copy-start.1 = (bf16[128,2048]{1,0:T(8,128)(2,1)S(1)}, bf16[128,2048]{1,0:T(8,128)(2,1)}, u32[]{:S(2)}) copy-start(bf16[128,2048]{1,0:T(8,128)(2,1)} %get-tuple-element.55) | copy-start | bytes 1572868
Sparse Core Ops, SparseCore 0:
  336.1 140.9 all-reduce.5
  480.3 130.7 all-reduce.3
